TPU v7x, 32 devices: a whole 2x2x4 slice. The times are simulated.
32 devices in a mesh: section: 4 (over z), tensor: 4 (over y, x), dp: 2 (over core).
Axes of the slice: x: 2, y: 2, z: 4, core: 2. Of those that a mesh axis runs over, the one named last changes fastest.
Arguments:
- section_input: bfloat16 [4, 256, 4096], P('section', 'dp', 'tensor'), parts along dimension 1, may hold values from -6 to 6
- stash_pool: bfloat16 [4, 2, 256, 4096], P('section', None, 'dp', 'tensor'), parts along dimension 2, may hold values from -6 to 6
- reload_slot: int32 [4], P('section'), may hold values from 0 to 1
- cotangent: bfloat16 [4, 256, 4096], P('section', 'dp', 'tensor'), parts along dimension 1, may hold values from -6 to 6
- norm_gain: float32 [4, 4096], P('section', 'tensor'), may hold values from 0.5 to 6
- query_weight: bfloat16 [4, 4096, 4096], P('section', None, 'tensor'), may hold values from -0.09375 to 0.09375
- kv_weight: bfloat16 [4, 4096, 1024], P('section', 'tensor'), may hold values from -0.09375 to 0.09375
- out_weight: bfloat16 [4, 4096, 4096], P('section', 'tensor'), may hold values from -0.09375 to 0.09375
Outputs:
- next_input: bfloat16 [4, 256, 4096], P('section', 'dp', 'tensor'), parts along dimension 1
- received_stash: bfloat16 [4, 256, 4096], P('section', 'dp', 'tensor'), parts along dimension 1
- input_grad: bfloat16 [4, 256, 4096], P('section', 'dp', 'tensor'), parts along dimension 1
There are 2 independent parts, one for each index of `dp`. A program takes and returns all parts, laid end to end along the dimension named above; an argument that names none is the same for every part. Nothing has to cross between parts.
All inputs are finite; a program needn't handle non-finite values.
Results may differ from a plain program's by a relative error of at most 0.024.
The roundings to bfloat16 on the way count: a program that leaves them out, or rounds other values in their place, can miss the bound.
Values may be sent and summed in bfloat16 or wider, within the bound.
A program may use at most 64 MiB of HBM per device.

v0:
```python
import jax
import jax.numpy as jnp
from jax import lax
from jax.sharding import PartitionSpec as P

HEADS = 32
KVH = 4
HD = 128


norm_eps = 1e-05


def passed_along(block, axis, distance):
    devices = range(lax.axis_size(axis))
    route = [(i - distance, i) for i in devices if i - distance in devices]
    return lax.ppermute(block, axis, route)


def from_partner(value, axis, distance):
    mask = 2**distance
    pairs = [(source, source ^ mask) for source in range(lax.axis_size(axis))]
    return lax.ppermute(value, axis, pairs)


def rope_tables(row_total, head_width):
    half_width = head_width // 2
    inverse = 10000.0 ** (-2.0 * jnp.arange(half_width, dtype=jnp.float32) / head_width)
    angles = jnp.arange(row_total, dtype=jnp.float32)[:, None] * inverse[None, :]
    return (jnp.cos(angles)[:, None, :], jnp.sin(angles)[:, None, :])


def rotate(values, cos_table, sin_table):
    half_width = values.shape[-1] // 2
    first_half = values[..., :half_width]
    second_half = values[..., half_width:]
    return jnp.concatenate(
        [
            first_half * cos_table - second_half * sin_table,
            second_half * cos_table + first_half * sin_table,
        ],
        axis=-1,
    )


def unrotate(values, cos_table, sin_table):
    half_width = values.shape[-1] // 2
    first_half = values[..., :half_width]
    second_half = values[..., half_width:]
    return jnp.concatenate(
        [
            first_half * cos_table + second_half * sin_table,
            second_half * cos_table - first_half * sin_table,
        ],
        axis=-1,
    )


def feature_total(partial_value):
    return lax.psum(partial_value, "tensor")


def gather_features(local_cols):
    return lax.all_gather(local_cols, "tensor", axis=1, tiled=True)


def tensor_total(partial_value):
    return lax.psum(partial_value, "tensor")


def pipe(values_out, offset):
    return passed_along(values_out, "section", offset)


def contract_last(left_side, right_side):
    return lax.dot_general(
        left_side, right_side, (((1,), (1,)), ((), ())), preferred_element_type=jnp.float32
    )


def group_kv(normed_cols, kv_w, group_index):
    token_count = normed_cols.shape[0]
    partial_value = jnp.dot(normed_cols, kv_w, preferred_element_type=jnp.float32)
    kv_all = tensor_total(partial_value).reshape(token_count, 2, KVH, HD)
    key_head = lax.dynamic_index_in_dim(kv_all[:, 0], group_index, 1, keepdims=False)
    value_head = lax.dynamic_index_in_dim(kv_all[:, 1], group_index, 1, keepdims=False)
    return (key_head, value_head)


def norm_factor(rows_wide):
    full_width = rows_wide.shape[1] * lax.axis_size("tensor")
    total = feature_total(jnp.sum(rows_wide * rows_wide, axis=-1, keepdims=True))
    return lax.rsqrt(total / full_width + norm_eps)


def local_heads(normed_cols, query_w, kv_w, cos_table, sin_table, group_index):
    gathered = gather_features(normed_cols)
    token_count = gathered.shape[0]
    key_wide, value_wide = group_kv(normed_cols, kv_w, group_index)
    key_head = rotate(key_wide[:, None, :], cos_table, sin_table).astype(jnp.bfloat16)[:, 0]
    value_head = value_wide.astype(jnp.bfloat16)
    query_heads = jnp.dot(gathered, query_w, preferred_element_type=jnp.float32).reshape(
        token_count, -1, HD
    )
    query_heads = (rotate(query_heads, cos_table, sin_table) * HD ** (-0.5)).astype(jnp.bfloat16)
    scores = jnp.einsum("thd,sd->hts", query_heads, key_head, preferred_element_type=jnp.float32)
    causal = jnp.arange(token_count)[:, None] >= jnp.arange(token_count)[None, :]
    scores = jnp.where(causal[None], scores, -1e30)
    shifted = jnp.exp(scores - jnp.max(scores, axis=-1, keepdims=True))
    softmax_probs = shifted / jnp.sum(shifted, axis=-1, keepdims=True)
    prob_weights = softmax_probs.astype(jnp.bfloat16)
    attended = jnp.einsum(
        "hts,sd->thd", prob_weights, value_head, preferred_element_type=jnp.float32
    )
    attended = attended.astype(jnp.bfloat16).reshape(token_count, -1)
    return (query_heads, key_head, value_head, softmax_probs, prob_weights, attended)


def per_device(
    section_input,
    stash_pool,
    reload_slot,
    cotangent,
    norm_gain,
    query_weight,
    kv_weight,
    out_weight,
):
    token_rows = section_input[0]
    cot_rows = cotangent[0]
    gain_row = norm_gain[0]
    query_w = query_weight[0]
    kv_w = kv_weight[0]
    out_w = out_weight[0]
    section_count = lax.axis_size("section")
    section_pos = lax.axis_index("section")
    is_early = section_pos < section_count // 2
    tensor_pos = lax.axis_index("tensor")
    local_width = token_rows.shape[1]
    column_start = tensor_pos * local_width
    heads_here = query_w.shape[1] // HD
    group_index = tensor_pos * heads_here // (HEADS // KVH)
    token_count = token_rows.shape[0]
    full_width = local_width * lax.axis_size("tensor")
    cos_table, sin_table = rope_tables(token_count, HD)
    rows_wide = token_rows.astype(jnp.float32)
    normed = (rows_wide * norm_factor(rows_wide) * gain_row).astype(jnp.bfloat16)
    attended = local_heads(normed, query_w, kv_w, cos_table, sin_table, group_index)[5]
    out_term = jnp.dot(attended, out_w, preferred_element_type=jnp.float32)
    summed = lax.psum(out_term.astype(jnp.bfloat16), "tensor").astype(jnp.float32)
    own_cols = lax.dynamic_slice_in_dim(summed, column_start, local_width, 1)
    layer_out = (rows_wide + own_cols).astype(jnp.bfloat16)
    next_input = pipe(layer_out, 1)
    picked = lax.dynamic_index_in_dim(stash_pool[0], reload_slot[0], 0, keepdims=False)
    travel = jnp.where(is_early, token_rows, picked)
    bit_count = section_count.bit_length() - 1
    for bit_index in range(bit_count):
        travel = from_partner(travel, "section", bit_index)
    back_input = jnp.where(is_early, travel, token_rows)
    back_wide = back_input.astype(jnp.float32)
    factor = norm_factor(back_wide)
    back_normed = (back_wide * factor * gain_row).astype(jnp.bfloat16)
    query_heads, key_head, value_head, softmax_probs, prob_weights, _ = local_heads(
        back_normed, query_w, kv_w, cos_table, sin_table, group_index
    )
    cot_whole = gather_features(cot_rows)
    grad_out = (
        contract_last(cot_whole, out_w).astype(jnp.bfloat16).reshape(token_count, heads_here, HD)
    )
    grad_probs = jnp.einsum("thd,sd->hts", grad_out, value_head, preferred_element_type=jnp.float32)
    row_delta = jnp.sum(softmax_probs * grad_probs, axis=-1, keepdims=True)
    grad_scores = (softmax_probs * (grad_probs - row_delta)).astype(jnp.bfloat16)
    grad_query = jnp.einsum(
        "hts,sd->thd", grad_scores, key_head, preferred_element_type=jnp.float32
    )
    grad_query = (
        (unrotate(grad_query, cos_table, sin_table) * HD ** (-0.5))
        .astype(jnp.bfloat16)
        .reshape(token_count, -1)
    )
    grad_key = jnp.einsum(
        "hts,thd->sd", grad_scores, query_heads, preferred_element_type=jnp.float32
    )
    grad_key = unrotate(grad_key[:, None, :], cos_table, sin_table)[:, 0]
    grad_value = jnp.einsum(
        "hts,thd->sd", prob_weights, grad_out, preferred_element_type=jnp.float32
    )
    placed = jnp.zeros((token_count, 2, KVH, HD), jnp.float32)
    placed = lax.dynamic_update_slice(
        placed, jnp.stack([grad_key, grad_value], axis=1)[:, :, None, :], (0, 0, group_index, 0)
    )
    grad_kv = tensor_total(placed.reshape(token_count, 2 * KVH * HD)).astype(jnp.bfloat16)
    query_cols = lax.psum_scatter(
        contract_last(grad_query, query_w).astype(jnp.bfloat16),
        "tensor",
        scatter_dimension=1,
        tiled=True,
    ).astype(jnp.float32)
    grad_normed = query_cols + contract_last(grad_kv, kv_w)
    scaled = grad_normed * gain_row
    mixed_mean = feature_total(jnp.sum(scaled * back_wide, axis=-1, keepdims=True)) / full_width
    grad_rows = factor * scaled - back_wide * factor * factor * factor * mixed_mean
    grad_local = (cot_rows.astype(jnp.float32) + grad_rows).astype(jnp.bfloat16)
    input_grad = pipe(grad_local, -1)
    return (next_input[None], travel[None], input_grad[None])


def solution(mesh):
    return jax.shard_map(
        per_device,
        mesh=mesh,
        in_specs=(
            P("section", "dp", "tensor"),
            P("section", None, "dp", "tensor"),
            P("section"),
            P("section", "dp", "tensor"),
            P("section", "tensor"),
            P("section", None, "tensor"),
            P("section", "tensor", None),
            P("section", "tensor", None),
        ),
        out_specs=(
            P("section", "dp", "tensor"),
            P("section", "dp", "tensor"),
            P("section", "dp", "tensor"),
        ),
        check_vma=False,
    )
```

profile of v0, /device:TPU:0, one launch (start us, length us, event | category | flops | bytes accessed | tf_op | source)
XLA Modules:
  0.0 384.2 jit_solution(4946838898520985108)
XLA Ops:
  9.1 3.1 collective-permute-start.1
  12.2 6.3 %collective-permute-done.1 = bf16[128,1024]{1,0:T(8,128)(2,1)S(1)} collective-permute-done((bf16[128,1024]{1,0:T(8,128)(2,1)S(1)}, bf16[128,1024]{1,0:T(8,128)(2,1)S(1)}, u32[]{:S(2)}, u32[]{:S(2)}) %collective-permute-start.1) | collective-permute-done | bytes 262176 | tf_op jit(solution)/shard_map/ppermute | solution.py:23
  18.5 2.8 collective-permute-start.2
  21.2 11.3 %collective-permute-done.2 = bf16[128,1024]{1,0:T(8,128)(2,1)S(1)} collective-permute-done((bf16[128,1024]{1,0:T(8,128)(2,1)S(1)}, bf16[128,1024]{1,0:T(8,128)(2,1)S(1)}, u32[]{:S(2)}, u32[]{:S(2)}) %collective-permute-start.2) | collective-permute-done | bytes 262176 | tf_op jit(solution)/shard_map/ppermute | solution.py:23
  34.9 9.7 %psum.52 = f32[128,1]{0,1:T(1,128)S(1)} all-reduce(f32[128,1]{0,1:T(1,128)S(1)} %bitcast.188), channel_id=1, replica_groups=mesh['section'=4,'tensor'=4,'dp'=2] {'tensor'}, use_global_device_ids=true, to_apply=%region_7.8 | all-reduce | flops 128 | bytes 1024 | tf_op jit(solution)/shard_map/psum | solution.py:60
  51.0 11.2 %copy.57 = bf16[1024,4096]{1,0:T(8,128)(2,1)} copy(bf16[1024,4096]{0,1:T(8,128)(2,1)} %bitcast.171) | data formatting | bytes 16777216 | tf_op jit(solution)/shard_map/dot_general | solution.py:102
  62.5 31.7 %all-reduce.10.cloned.1.call-done = f32[128,2,4,128]{3,0,2,1:T(8,128)} async-done(((f32[128,2,4,128]{3,0,2,1:T(8,128)}), f32[128,2,4,128]{3,0,2,1:T(8,128)}) %all-reduce.10.cloned.1.call-update) | async-done | bytes 524304 | tf_op jit(solution)/shard_map/psum | solution.py:68
  97.1 25.6 %all-gather.9.cloned.1.call-done = bf16[1,128,4096]{2,1,0:T(8,128)(2,1)} async-done(((bf16[1,128,1024]{2,1,0:T(8,128)(2,1)}), bf16[1,128,4096]{2,1,0:T(8,128)(2,1)}) %all-gather.9.cloned.1.call-update) | async-done | bytes 1048592 | tf_op jit(solution)/shard_map/all_gather | solution.py:64
  122.7 6.6 %fusion.32 = bf16[128,1024]{1,0:T(8,128)(2,1)S(1)} fusion(bf16[1,1024,4096]{2,1,0:T(8,128)(2,1)} %param.15, bf16[1,128,4096]{2,1,0:T(8,128)(2,1)} %all-gather.9.cloned.1.call-done), kind=kOutput, calls=%fused_computation.28 | convolution fusion | flops 1073872896 | bytes 9699328 | tf_op jit(solution)/shard_map/dot_general | solution.py:76
  129.5 22.3 %all-gather.7.cloned.1.call-done = bf16[128,4096]{1,0:T(8,128)(2,1)} async-done(((bf16[128,1024]{1,0:T(8,128)(2,1)}), bf16[128,4096]{1,0:T(8,128)(2,1)}) %all-gather.7.cloned.1.call-update) | async-done | bytes 1048592 | tf_op jit(solution)/shard_map/all_gather | solution.py:64
  151.8 6.0 %fusion.36 = f32[128,8,128]{0,2,1:T(8,128)S(1)} fusion(bf16[8,128,4096]{2,1,0:T(8,128)(2,1)} %bitcast.169, bf16[128,4096]{1,0:T(8,128)(2,1)} %all-gather.7.cloned.1.call-done), kind=kOutput, calls=%fused_computation.33 | convolution fusion | flops 1073741824 | bytes 9961472 | tf_op jit(solution)/shard_map/dot_general | solution.py:102
  161.6 7.4 %fusion.8 = bf16[128,4096]{1,0:T(8,128)(2,1)} fusion(bf16[128,1024]{0,1:T(8,128)(2,1)S(1)} %bitcast.174, bf16[1,4096,1024]{2,1,0:T(8,128)(2,1)} %param.13), kind=kOutput, calls=%fused_computation.8 | convolution fusion | flops 1074266112 | bytes 9699328 | tf_op jit(solution)/shard_map/dot_general | solution.py:76
  172.6 34.9 %all-reduce.11 = bf16[128,1024]{0,1:T(8,128)(2,1)S(1)} all-reduce(f32[128,1024]{0,1:T(8,128)S(1)} %bitcast.173), channel_id=1, replica_groups=mesh['section'=4,'tensor'=4,'dp'=2] {'tensor'}, use_global_device_ids=true, to_apply=%region_13.14 | all-reduce | flops 131072 | bytes 786432 | tf_op jit(solution)/shard_map/psum | solution.py:68
  207.6 1.9 fusion.53
  209.4 8.2 %all-reduce = (f32[128,1]{0,1:T(1,128)S(1)}, f32[128,1]{0,1:T(1,128)S(1)}) all-reduce(f32[128,1]{0,1:T(1,128)S(1)} %bitcast.187, f32[128,1]{0,1:T(1,128)S(1)} %bitcast.186), channel_id=1, replica_groups=mesh['section'=4,'tensor'=4,'dp'=2] {'tensor'}, use_global_device_ids=true, to_apply=%region_1.2 | all-reduce | flops 256 | bytes 2048 | tf_op jit(solution)/shard_map/psum | solution.py:60
  220.4 45.1 %all-reduce.6.cloned.1.call-done = f32[128,2,4,128]{0,3,2,1:T(8,128)} async-done(((f32[128,2,4,128]{0,3,2,1:T(8,128)}), f32[128,2,4,128]{0,3,2,1:T(8,128)}) %all-reduce.6.cloned.1.call-update) | async-done | bytes 524304 | tf_op jit(solution)/shard_map/psum | solution.py:68
  268.5 26.1 %all-gather.5.cloned.1.call-done = bf16[128,4096]{1,0:T(8,128)(2,1)} async-done(((bf16[128,1024]{1,0:T(8,128)(2,1)}), bf16[128,4096]{1,0:T(8,128)(2,1)}) %all-gather.5.cloned.1.call-update) | async-done | bytes 1048592 | tf_op jit(solution)/shard_map/all_gather | solution.py:64
  294.6 6.0 %fusion.38 = f32[128,8,128]{0,2,1:T(8,128)S(1)} fusion(bf16[8,128,4096]{2,1,0:T(8,128)(2,1)} %bitcast.170, bf16[128,4096]{1,0:T(8,128)(2,1)} %all-gather.5.cloned.1.call-done), kind=kOutput, calls=%fused_computation.35 | convolution fusion | flops 1073741824 | bytes 9961472 | tf_op jit(solution)/shard_map/dot_general | solution.py:102
  304.5 2.2 convolution_convert_fusion
  306.7 5.8 %fusion.11 = bf16[128,4096]{1,0:T(8,128)(2,1)} fusion(bf16[128,1024]{0,1:T(8,128)(2,1)} %bitcast.176, bf16[1,1024,4096]{2,1,0:T(8,128)(2,1)} %param.15), kind=kOutput, calls=%fused_computation.9 | convolution fusion | flops 1074266112 | bytes 9699328 | tf_op jit(solution)/shard_map/dot_general | solution.py:149
  312.6 1.9 fusion.47
  315.8 49.5 %all-reduce.8.cloned.1.call-done = bf16[128,4096]{1,0:T(8,128)(2,1)} async-done(((bf16[128,4096]{1,0:T(8,128)(2,1)}), bf16[128,4096]{1,0:T(8,128)(2,1)}) %all-reduce.8.cloned.1.call-update) | async-done | bytes 1048592 | tf_op jit(solution)/shard_map/psum | solution.py:150
  366.3 3.4 collective-permute-start
  369.7 5.5 %collective-permute-done = bf16[128,1024]{1,0:T(8,128)(2,1)S(1)} collective-permute-done((bf16[128,1024]{1,0:T(8,128)(2,1)S(1)}, bf16[128,1024]{1,0:T(8,128)(2,1)S(1)}, u32[]{:S(2)}, u32[]{:S(2)}) %collective-permute-start) | collective-permute-done | bytes 262176 | tf_op jit(solution)/shard_map/ppermute | solution.py:17
  (93 shorter events, 34.3 us)
Async XLA Ops:
  7.2 38.9 %copy-start = (bf16[1,1024,1024]{2,1,0:T(8,128)(2,1)S(1)}, bf16[1,1024,1024]{2,1,0:T(8,128)(2,1)}, u32[]{:S(2)}) copy-start(bf16[1,1024,1024]{2,1,0:T(8,128)(2,1)} %param.14) | copy-start | bytes 6291460
  7.2 87.0 %all-reduce.10.cloned.1.call-start = ((), (), s32[]{:S(2)}) async-start(), calls=%async_computation.4 | async-start | bytes 1048576 | tf_op jit(solution)/shard_map/psum | solution.py:68
  9.1 9.4 %collective-permute-start.1 = (bf16[128,1024]{1,0:T(8,128)(2,1)S(1)}, bf16[128,1024]{1,0:T(8,128)(2,1)S(1)}, u32[]{:S(2)}, u32[]{:S(2)}) collective-permute-start(bf16[128,1024]{1,0:T(8,128)(2,1)S(1)} %bitcast_select_fusion), channel_id=1, source_target_pairs={{0,8},{8,0},{16,24},{24,16},{1,9},{9,1},{17,25},{25,17},{2,10},{10... | collective-permute-start | bytes 786440 | tf_op jit(solution)/shard_map/ppermute | solution.py:23
  18.5 14.0 %collective-permute-start.2 = (bf16[128,1024]{1,0:T(8,128)(2,1)S(1)}, bf16[128,1024]{1,0:T(8,128)(2,1)S(1)}, u32[]{:S(2)}, u32[]{:S(2)}) collective-permute-start(bf16[128,1024]{1,0:T(8,128)(2,1)S(1)} %collective-permute-done.1), channel_id=1, source_target_pairs={{0,16},{8,24},{16,0},{24,8},{1,17},{9,25},{17,1},{25,9},{2,18},{10... | collective-permute-start | bytes 786440 | tf_op jit(solution)/shard_map/ppermute | solution.py:23
  46.0 4.2 %copy-start.2 = (bf16[128,1024]{1,0:T(8,128)(2,1)}, bf16[128,1024]{1,0:T(8,128)(2,1)S(1)}, u32[]{:S(2)}) copy-start(bf16[128,1024]{1,0:T(8,128)(2,1)S(1)} %fusion.42) | copy-start | bytes 786436
  49.5 73.2 %all-gather.9.cloned.1.call-start = ((), (), s32[]{:S(2)}) async-start(), calls=%async_computation.7 | async-start | bytes 1310720 | tf_op jit(solution)/shard_map/all_gather | solution.py:64
  50.2 101.6 %all-gather.7.cloned.1.call-start = ((), (), s32[]{:S(2)}) async-start(), calls=%async_computation.5 | async-start | bytes 1310720 | tf_op jit(solution)/shard_map/all_gather | solution.py:64
  50.9 156.6 %reduce-scatter.2.cloned.1.call-start = ((), (), s32[]{:S(2)}) async-start(), calls=%async_computation.6 | async-start | bytes 1310720 | tf_op jit(solution)/shard_map/reduce_scatter | solution.py:193
  62.2 34.8 %copy-start.9 = (f32[64]{0:T(128)}, f32[64]{0:T(128)S(1)}, u32[]{:S(2)}) copy-start(f32[64]{0:T(128)S(1)} %multiply_power_fusion) | copy-start | bytes 772
  62.3 95.7 %copy-start.8 = (pred[128,128]{0,1:T(8,128)(4,1)}, pred[128,128]{0,1:T(8,128)(4,1)S(1)}, u32[]{:S(2)}) copy-start(pred[128,128]{0,1:T(8,128)(4,1)S(1)} %iota_compare_fusion) | copy-start | bytes 49156
  158.9 1.1 copy-start.6
  158.9 10.4 %copy-start.10 = (f32[64]{0:T(128)S(1)}, f32[64]{0:T(128)}, u32[]{:S(2)}) copy-start(f32[64]{0:T(128)} %copy-done.9) | copy-start | bytes 772
  159.0 10.7 %copy-start.11 = (f32[8,128]{1,0:T(8,128)S(1)}, f32[8,128]{1,0:T(8,128)}, u32[]{:S(2)}) copy-start(f32[8,128]{1,0:T(8,128)} %get-tuple-element.22) | copy-start | bytes 12292
  161.5 46.0 %copy-start.7 = (f32[1,1024]{1,0:T(1,128)S(1)}, f32[1,1024]{1,0:T(1,128)}, u32[]{:S(2)}) copy-start(f32[1,1024]{1,0:T(1,128)} %param.12) | copy-start | bytes 12292
  161.6 47.8 %copy-start.14 = (f32[128]{0:T(128)S(1)}, f32[128]{0:T(128)}, u32[]{:S(2)}) copy-start(f32[128]{0:T(128)} %get-tuple-element.13) | copy-start | bytes 1540
  161.6 56.0 %copy-start.1 = (bf16[1,128,1024]{2,1,0:T(8,128)(2,1)S(1)}, bf16[1,128,1024]{2,1,0:T(8,128)(2,1)}, u32[]{:S(2)}) copy-start(bf16[1,128,1024]{2,1,0:T(8,128)(2,1)} %param.8) | copy-start | bytes 786436
  169.0 96.4 %all-reduce.6.cloned.1.call-start = ((), (), s32[]{:S(2)}) async-start(), calls=%async_computation.1 | async-start | bytes 1048576 | tf_op jit(solution)/shard_map/psum | solution.py:68
  219.5 75.1 %all-gather.5.cloned.1.call-start = ((), (), s32[]{:S(2)}) async-start(), calls=%async_computation.2 | async-start | bytes 1310720 | tf_op jit(solution)/shard_map/all_gather | solution.py:64
  220.4 144.9 %all-reduce.8.cloned.1.call-start = ((), (), s32[]{:S(2)}) async-start(), calls=%async_computation.3 | async-start | bytes 2097152 | tf_op jit(solution)/shard_map/psum | solution.py:150
  300.7 0.7 copy-start.3
  304.5 8.1 %copy-start.13 = (f32[128]{0:T(128)S(1)}, f32[128]{0:T(128)}, u32[]{:S(2)}) copy-start(f32[128]{0:T(128)} %copy-done.12) | copy-start | bytes 1540
  306.7 69.2 %copy-start.5 = (bf16[128,1024]{1,0:T(8,128)(2,1)S(1)}, bf16[128,1024]{1,0:T(8,128)(2,1)}, u32[]{:S(2)}) copy-start(bf16[128,1024]{1,0:T(8,128)(2,1)} %copy-done.4) | copy-start | bytes 786436
  314.5 55.2 %collective-permute-start.3 = (bf16[128,1024]{1,0:T(8,128)(2,1)}, bf16[128,1024]{1,0:T(8,128)(2,1)S(1)}, u32[]{:S(2)}, u32[]{:S(2)}) collective-permute-start(bf16[128,1024]{1,0:T(8,128)(2,1)} %fusion.47), channel_id=1, source_target_pairs={{8,0},{16,8},{24,16},{9,1},{17,9},{25,17},{10,2},{18,10},{26,18},{... | collective-permute-start | bytes 786440 | tf_op jit(solution)/shard_map/ppermute | solution.py:17
  366.3 8.9 %collective-permute-start = (bf16[128,1024]{1,0:T(8,128)(2,1)S(1)}, bf16[128,1024]{1,0:T(8,128)(2,1)S(1)}, u32[]{:S(2)}, u32[]{:S(2)}) collective-permute-start(bf16[128,1024]{1,0:T(8,128)(2,1)S(1)} %fusion.51), channel_id=1, source_target_pairs={{0,8},{8,16},{16,24},{1,9},{9,17},{17,25},{2,10},{10,18},{18,26},{... | collective-permute-start | bytes 786440 | tf_op jit(solution)/shard_map/ppermute | solution.py:17
  (2 other events, 1.3 us)
Sparse Core Ops, SparseCore 0:
  49.6 44.5 all-reduce.9
  96.0 26.6 all-gather.8
  125.1 26.6 all-gather.6
  169.2 34.5 reduce-scatter.1
  219.6 45.8 all-reduce.5
  267.9 26.6 all-gather.4
  312.7 52.5 all-reduce.7
where the time goes:
time: 385 us; the launch traced here: 384 us
  waiting for transfers between devices  225 us (58%)
  blocking collectives  52.9 us (14%)
  matrix products  46.5 us (12%)
  local copies, waits for them, and re-layouts  23.2 us (6%)
  between operations  15.3 us (4%)
  starting transfers between devices  10.8 us (3%)
  other arithmetic  10.7 us (3%)
    psum x2, waiting for transfers between devices, tensor_total(): return lax.psum(partial_value, 'tensor')  76.8 us
    all_gather x3, waiting for transfers between devices, gather_features(): return lax.all_gather(local_cols, 'tensor', axis=1, tiled=True)  74 us
    psum x1, waiting for transfers between devices, per_device(): lax.psum(out_term.astype(jnp.bfloat16), 'tensor').astype(jnp.float32)  49.5 us
    psum x1, blocking collectives, tensor_total(): return lax.psum(partial_value, 'tensor')  34.9 us
    psum x2, blocking collectives, feature_total(): return lax.psum(partial_value, 'tensor')  17.9 us
    ppermute x2, waiting for transfers between devices, from_partner(): return lax.ppermute(value, axis, pairs)  17.6 us
    dot_general x3, matrix products, contract_last(): lax.dot_general(left_side, right_side, (((1,), (1,)), ((), ())), preferre...  15.9 us
    dot_general x2, matrix products, local_heads(): jnp.dot(gathered, query_w, preferred_element_type=jnp.float32)  12.1 us
  transfers between devices with their start and end apart: 11, of which 9 were waited for; matrix products, arithmetic and copies ran while one was open for 8% of the time, Pallas kernels for 0%

commit v1 on v0

v1 whole, which is shorter than its diff:
```python
import functools

import jax
import jax.numpy as jnp
import numpy as np
from jax import lax
from jax.experimental import pallas as pl
from jax.experimental.pallas import tpu as pltpu
from jax.sharding import PartitionSpec as P

HEADS = 32
KVH = 4
HD = 128
PAIR = 2
TILE = 256
SUMROWS = 8
ZCHUNKS = 4

norm_eps = 1e-05
f32 = jnp.float32
bf16 = jnp.bfloat16


def rope_constants(tokens):
    half = HD // 2
    inverse = np.float32(10000.0) ** (
        np.float32(-2.0) * np.arange(half, dtype=np.float32) / np.float32(HD)
    )
    angles = np.arange(tokens, dtype=np.float32)[:, None] * inverse[None, :].astype(np.float32)
    cos, sin = np.cos(angles), np.sin(angles)
    return (
        np.concatenate([cos, cos], axis=1).astype(np.float32),
        np.concatenate([-sin, sin], axis=1).astype(np.float32),
    )


def flipped(index, bits):
    place = 1
    while place <= bits:
        if bits & place:
            bit = lax.rem(lax.div(index, place), 2)
            index = index + place * (1 - 2 * bit)
        place *= 2
    return index


def dot_nn(a, b):
    return jnp.dot(a, b, preferred_element_type=f32)


def dot_nt(a, b):
    return lax.dot_general(a, b, (((1,), (1,)), ((), ())), preferred_element_type=f32)


def dot_tn(a, b):
    return lax.dot_general(a, b, (((0,), (0,)), ((), ())), preferred_element_type=f32)


def layer_kernel(
    ways,
    sections,
    slot_ref,
    x_ref,
    stash_ref,
    cot_ref,
    gain_ref,
    cos_ref,
    sin_ref,
    qw_hbm,
    kvw_hbm,
    ow_hbm,
    next_ref,
    travel_ref,
    igrad_ref,
    qw,
    kvw,
    ow,
    xg,
    bg,
    cg,
    gg,
    fn,
    bn,
    fact,
    qf,
    qb,
    go,
    att,
    gqb,
    kvf_p,
    kvf_r,
    kvb_p,
    kvb_r,
    out_p,
    out_s,
    out_r,
    gq_p,
    gq_s,
    gq_r,
    gk_s,
    gk_r,
    gk_acc,
    gk_full,
    trav,
    lo,
    gl,
    scaled,
    msum,
    wsem,
    ssem,
    rsem,
):
    tokens, width = x_ref.shape
    heads_here = qw.shape[1] // HD
    model = width * ways
    half = tokens // 2
    upper, lower = pl.ds(0, half), pl.ds(half, half)
    me = lax.axis_index("tensor")
    sec = lax.axis_index("section")
    early = sec < sections // 2
    has_prev = sec > 0
    has_next = sec < sections - 1
    mirror = sections - 1 - sec
    prev = jnp.maximum(sec - 1, 0)
    nxt = jnp.minimum(sec + 1, sections - 1)
    peers = [flipped(me, k) for k in range(ways)]
    rows_of = [pl.ds(pl.multiple_of(p * width, width), width) for p in peers]
    relay = ways == 4
    per_group = ways // KVH
    groups = [lax.div(p, per_group) for p in peers]

    loads = [
        pltpu.make_async_copy(a, b, wsem.at[i])
        for i, (a, b) in enumerate(((kvw_hbm, kvw), (qw_hbm, qw), (ow_hbm, ow)))
    ]
    for load in loads:
        load.start()

    used = []
    pending = []

    def send(src, dst, axis, peer, start=True):
        i = len(used)
        used.append(i)
        copy = pltpu.make_async_remote_copy(
            src_ref=src,
            dst_ref=dst,
            send_sem=ssem.at[i],
            recv_sem=rsem.at[i],
            device_id={axis: peer},
            device_id_type=pl.DeviceIdType.MESH,
        )
        if start:
            copy.start()
            pending.append(copy)
        return copy

    def to_peer(k, src, dst):
        return send(src, dst, "tensor", peers[k])

    barrier = pltpu.get_barrier_semaphore()

    def greet(axis, peer):
        pl.semaphore_signal(
            barrier, inc=1, device_id={axis: peer}, device_id_type=pl.DeviceIdType.MESH
        )

    for k in range(1, ways):
        greet("tensor", peers[k])
    greet("section", mirror)

    @pl.when(has_prev)
    def _():
        greet("section", prev)

    @pl.when(has_next)
    def _():
        greet("section", nxt)

    @pl.when(early)
    def _():
        trav[...] = x_ref[...]

    @pl.when(jnp.logical_not(early))
    def _():
        trav[...] = stash_ref[slot_ref[0]]

    xg[0] = x_ref[...]
    cg[0] = cot_ref[...]
    gg[0] = jnp.broadcast_to(gain_ref[...], gg.shape[1:])

    pl.semaphore_wait(barrier, ways + jnp.minimum(sec, 1) + jnp.minimum(sections - 1 - sec, 1))

    def gather_start(buf):
        if relay:
            return [to_peer(k, buf.at[0], buf.at[k]) for k in (1, 2)]
        return [to_peer(k, buf.at[0], buf.at[k]) for k in range(1, ways)]

    def gather_pass_on(buf, copies):
        if not relay:
            return copies
        copies[0].wait_recv()
        first = to_peer(2, buf.at[1, upper], buf.at[3, upper])
        copies[1].wait_recv()
        second = to_peer(1, buf.at[2, lower], buf.at[3, lower])
        return [first, second]

    def finish(copies):
        for copy in copies:
            copy.wait_recv()

    order = (3, 1, 2, 0) if relay else tuple(range(1, ways)) + (0,)

    def reduce_send(k, stage, land):
        if k == 0:
            return []
        if not relay:
            return [to_peer(k, stage.at[k], land.at[k])]
        if k == 3:
            return [
                to_peer(1, stage.at[3, upper], land.at[2, upper]),
                to_peer(2, stage.at[3, lower], land.at[1, lower]),
            ]
        if k == 1:
            return [to_peer(1, stage.at[1, upper], land.at[0, upper])]
        return [to_peer(2, stage.at[2, lower], land.at[0, lower])]

    def reduce_pass_on(copies, part, stage, land):
        if not relay:
            return copies
        copies[0].wait_recv()
        stage[2, upper] = (part[2, upper] + land[2, upper].astype(f32)).astype(stage.dtype)
        first = to_peer(2, stage.at[2, upper], land.at[3, upper])
        copies[1].wait_recv()
        stage[1, lower] = (part[1, lower] + land[1, lower].astype(f32)).astype(stage.dtype)
        second = to_peer(1, stage.at[1, lower], land.at[3, lower])
        return copies[2:] + [first, second]

    def reduced(part, land, rows, cols):
        total = part[0, rows, cols]
        for k in (0, 3) if relay else range(1, ways):
            total = total + land[k, rows, cols].astype(f32)
        return total

    def normalize(raw, out, keep):
        step = 16

        def body(i, carry):
            rows = pl.ds(pl.multiple_of(i * step, step), step)
            total = jnp.zeros((step, 1), f32)
            for k in range(ways):
                v = raw[k, rows, :].astype(f32)
                total = total + jnp.sum(v * v, axis=-1, keepdims=True)
            factor = lax.rsqrt(total / model + norm_eps)
            for k in range(ways):
                v = raw[k, rows, :].astype(f32)
                out[k, rows, :] = (v * factor * gg[k, 0:1, :]).astype(bf16)
            if keep:
                fact[rows, :] = jnp.broadcast_to(factor, (step, HD))
            return carry

        lax.fori_loop(0, tokens // step, body, 0)

    def kv_terms(normed, part, land):
        copies = []
        for k in order:
            key_cols = pl.ds(pl.multiple_of(groups[k] * HD, HD), HD)
            value_cols = pl.ds(pl.multiple_of((KVH + groups[k]) * HD, HD), HD)
            part[k, :, 0:HD] = dot_nn(normed[0], kvw[:, key_cols])
            part[k, :, HD : 2 * HD] = dot_nn(normed[0], kvw[:, value_cols])
            copies += reduce_send(k, part, land)
        return copies

    def rotate(u):
        return u * cos_ref[...] + pltpu.roll(u, HD // 2, 1) * sin_ref[...]

    def unrotate(u):
        return u * cos_ref[...] - pltpu.roll(u, HD // 2, 1) * sin_ref[...]

    per_tile = TILE // HD
    scale = HD ** (-0.5)

    def queries(normed, out):
        def body(n, carry):
            cols = pl.ds(pl.multiple_of(n * TILE, TILE), TILE)
            acc = dot_nn(normed[0], qw[rows_of[0], cols])
            for k in range(1, ways):
                acc = acc + dot_nn(normed[k], qw[rows_of[k], cols])
            for j in range(per_tile):
                head = acc[:, j * HD : (j + 1) * HD]
                out[n * per_tile + j] = (rotate(head) * scale).astype(bf16)
            return carry

        lax.fori_loop(0, heads_here // per_tile, body, 0)

    def key_value(part, land):
        everything = pl.ds(0, tokens)
        key = rotate(reduced(part, land, everything, pl.ds(0, HD))).astype(bf16)
        value = reduced(part, land, everything, pl.ds(HD, HD)).astype(bf16)
        return key, value

    span = PAIR * tokens
    position = lax.rem(lax.broadcasted_iota(jnp.int32, (span, tokens), 0), tokens)
    seen = position >= lax.broadcasted_iota(jnp.int32, (span, tokens), 1)

    def probabilities(q, key):
        scores = jnp.where(seen, dot_nt(q, key), -1e30)
        shifted = jnp.exp(scores - jnp.max(scores, axis=-1, keepdims=True))
        return shifted * (1.0 / jnp.sum(shifted, axis=-1, keepdims=True))

    def project(source, weight_tile, part, stage, land):
        copies = []
        for k in order:

            def body(n, carry, k=k):
                cols = pl.ds(pl.multiple_of(n * TILE, TILE), TILE)
                value = weight_tile(source, k, n)
                if not (relay and k == 3):
                    part[k, :, cols] = value
                if k:
                    stage[k, :, cols] = value.astype(bf16)
                return carry

            lax.fori_loop(0, width // TILE, body, 0)
            copies += reduce_send(k, stage, land)
        return copies

    def out_tile(source, k, n):
        cols = pl.ds(pl.multiple_of(peers[k] * width + n * TILE, TILE), TILE)
        return dot_nn(source[...], ow[:, cols])

    def query_tile(source, k, n):
        rows = pl.ds(pl.multiple_of(peers[k] * width + n * TILE, TILE), TILE)
        return dot_nt(source[...], qw[rows, :])

    travel_copy = send(trav, travel_ref, "section", mirror)
    gain_copies = [to_peer(k, gg.at[0], gg.at[k]) for k in range(1, ways)]
    x_copies = gather_start(xg)
    x_copies = gather_pass_on(xg, x_copies)

    travel_copy.wait_recv()

    @pl.when(early)
    def _():
        bg[0] = travel_ref[...]

    @pl.when(jnp.logical_not(early))
    def _():
        bg[0] = x_ref[...]

    b_copies = gather_start(bg)
    finish(gain_copies)
    finish(x_copies)
    normalize(xg, fn, False)
    loads[0].wait()
    kvf = kv_terms(fn, kvf_p, kvf_r)
    loads[1].wait()
    queries(fn, qf)
    kvf = reduce_pass_on(kvf, kvf_p, kvf_p, kvf_r)
    b_copies = gather_pass_on(bg, b_copies)
    c_copies = gather_start(cg)
    finish(kvf)
    key, value = key_value(kvf_p, kvf_r)
    for i in range(heads_here // PAIR):
        q = qf[PAIR * i : PAIR * (i + 1)].reshape(span, HD)
        weights = probabilities(q, key).astype(bf16)
        result = dot_nn(weights, value).astype(bf16)
        for j in range(PAIR):
            head = PAIR * i + j
            att[:, head * HD : (head + 1) * HD] = result[j * tokens : (j + 1) * tokens]

    finish(b_copies)
    normalize(bg, bn, True)
    kvb = kv_terms(bn, kvb_p, kvb_r)
    loads[2].wait()
    outs = project(att, out_tile, out_p, out_s, out_r)
    queries(bn, qb)
    kvb = reduce_pass_on(kvb, kvb_p, kvb_p, kvb_r)
    c_copies = gather_pass_on(cg, c_copies)
    outs = reduce_pass_on(outs, out_p, out_s, out_r)
    finish(c_copies)

    def cot_body(n, carry):
        rows = pl.ds(pl.multiple_of(n * TILE, TILE), TILE)
        acc = dot_nt(cg[0], ow[rows, rows_of[0]])
        for k in range(1, ways):
            acc = acc + dot_nt(cg[k], ow[rows, rows_of[k]])
        for j in range(per_tile):
            go[n * per_tile + j] = acc[:, j * HD : (j + 1) * HD].astype(bf16)
        return carry

    lax.fori_loop(0, heads_here // per_tile, cot_body, 0)
    finish(kvb)
    key, value = key_value(kvb_p, kvb_r)
    grad_key = jnp.zeros((tokens, HD), f32)
    grad_value = jnp.zeros((tokens, HD), f32)
    for i in range(heads_here // PAIR):
        q = qb[PAIR * i : PAIR * (i + 1)].reshape(span, HD)
        g = go[PAIR * i : PAIR * (i + 1)].reshape(span, HD)
        probs = probabilities(q, key)
        grad_probs = dot_nt(g, value)
        delta = jnp.sum(probs * grad_probs, axis=-1, keepdims=True)
        grad_scores = (probs * (grad_probs - delta)).astype(bf16)
        grad_q = dot_nn(grad_scores, key)
        for j in range(PAIR):
            head = PAIR * i + j
            turned = unrotate(grad_q[j * tokens : (j + 1) * tokens]) * scale
            gqb[:, head * HD : (head + 1) * HD] = turned.astype(bf16)
        grad_key = grad_key + dot_tn(grad_scores, q)
        grad_value = grad_value + dot_tn(probs.astype(bf16), g)
    gk_r[0, :, 0:HD] = unrotate(grad_key).astype(gk_r.dtype)
    gk_r[0, :, HD : 2 * HD] = grad_value.astype(gk_r.dtype)
    gk_copies = [to_peer(k, gk_r.at[0], gk_r.at[k]) for k in range(1, ways)]
    grads = project(gqb, query_tile, gq_p, gq_s, gq_r)

    finish(outs)
    chunk = tokens // ZCHUNKS
    next_copies = []
    for c in range(ZCHUNKS):
        rows = pl.ds(c * chunk, chunk)
        total = reduced(out_p, out_r, rows, pl.ds(0, width))
        lo[rows, :] = (x_ref[rows, :].astype(f32) + total).astype(bf16)
        copy = send(lo.at[rows], next_ref.at[rows], "section", nxt, start=False)
        pl.when(has_next)(copy.start)
        next_copies.append(copy)

    grads = reduce_pass_on(grads, gq_p, gq_s, gq_r)

    finish(gk_copies)
    if per_group == 1:
        for k in range(ways):
            key_cols = pl.ds(pl.multiple_of(groups[k] * HD, HD), HD)
            value_cols = pl.ds(pl.multiple_of((KVH + groups[k]) * HD, HD), HD)
            gk_full[:, key_cols] = gk_r[k, :, 0:HD]
            gk_full[:, value_cols] = gk_r[k, :, HD : 2 * HD]
    else:
        gk_acc[...] = jnp.zeros_like(gk_acc)
        for k in range(ways):
            key_cols = pl.ds(pl.multiple_of(groups[k] * HD, HD), HD)
            value_cols = pl.ds(pl.multiple_of((KVH + groups[k]) * HD, HD), HD)
            gk_acc[:, key_cols] += gk_r[k, :, 0:HD].astype(f32)
            gk_acc[:, value_cols] += gk_r[k, :, HD : 2 * HD].astype(f32)
        gk_full[...] = gk_acc[...].astype(bf16)
    for n in range(width // TILE):
        cols = pl.ds(n * TILE, TILE)
        gq_p[0, :, cols] += dot_nt(gk_full[...], kvw[cols, :])

    finish(grads)
    row_sum = jnp.zeros((tokens, 1), f32)
    for n in range(width // TILE):
        cols = pl.ds(n * TILE, TILE)
        part = reduced(gq_p, gq_r, pl.ds(0, tokens), cols) * gain_ref[:, cols]
        scaled[:, cols] = part
        row_sum = row_sum + jnp.sum(part * bg[0, :, cols].astype(f32), axis=-1, keepdims=True)
    eye = lax.broadcasted_iota(jnp.int32, (tokens, tokens), 0) == lax.broadcasted_iota(
        jnp.int32, (tokens, tokens), 1
    )
    as_row = jnp.sum(jnp.where(eye, row_sum, 0.0), axis=0, keepdims=True)
    msum[0] = jnp.broadcast_to(as_row, (SUMROWS, tokens))
    finish([to_peer(k, msum.at[0], msum.at[k]) for k in range(1, ways)])
    total = msum[0, 0:1, :]
    for k in range(1, ways):
        total = total + msum[k, 0:1, :]
    mean = jnp.sum(jnp.where(eye, total, 0.0), axis=1, keepdims=True) / model
    grad_copies = []
    for c in range(ZCHUNKS):
        rows = pl.ds(c * chunk, chunk)
        factor = fact[rows, 0:1]
        back = bg[0, rows, :].astype(f32)
        cube = factor * factor * factor * mean[c * chunk : (c + 1) * chunk]
        grad_rows = factor * scaled[rows, :] - back * cube
        gl[rows, :] = (cot_ref[rows, :].astype(f32) + grad_rows).astype(bf16)
        copy = send(gl.at[rows], igrad_ref.at[rows], "section", prev, start=False)
        pl.when(has_prev)(copy.start)
        grad_copies.append(copy)

    @pl.when(jnp.logical_not(has_prev))
    def _():
        next_ref[...] = jnp.zeros_like(next_ref)

    @pl.when(jnp.logical_not(has_next))
    def _():
        igrad_ref[...] = jnp.zeros_like(igrad_ref)

    for copy in pending:
        copy.wait_send()

    @pl.when(has_next)
    def _():
        for copy in next_copies:
            copy.wait_send()
        for copy in grad_copies:
            copy.wait_recv()

    @pl.when(has_prev)
    def _():
        for copy in next_copies:
            copy.wait_recv()
        for copy in grad_copies:
            copy.wait_send()


def copies_needed(ways):
    if ways == 4:
        return 1 + 3 + 3 * 4 + 4 * 6 + 3 + 3 + 2 * ZCHUNKS
    return 1 + (ways - 1) * 10 + 2 * ZCHUNKS


def per_device(
    ways,
    sections,
    section_input,
    stash_pool,
    reload_slot,
    cotangent,
    norm_gain,
    query_weight,
    kv_weight,
    out_weight,
):
    _, tokens, width = section_input.shape
    model = width * ways
    local = query_weight.shape[2]
    heads_here = local // HD
    cos_table, sin_table = rope_constants(tokens)
    grad_kv_type = bf16 if ways == KVH else f32
    copies = copies_needed(ways)
    vmem = pl.BlockSpec(memory_space=pltpu.VMEM)
    block = jax.ShapeDtypeStruct((tokens, width), bf16)
    gathered = pltpu.VMEM((ways, tokens, width), bf16)
    wide = pltpu.VMEM((ways, tokens, width), f32)
    kv_block = pltpu.VMEM((ways, tokens, 2 * HD), f32)
    head_block = pltpu.VMEM((heads_here, tokens, HD), bf16)
    flat = pltpu.VMEM((tokens, local), bf16)
    scratch = [
        pltpu.VMEM((model, local), bf16),
        pltpu.VMEM((width, 2 * KVH * HD), bf16),
        pltpu.VMEM((local, model), bf16),
        gathered,
        gathered,
        gathered,
        pltpu.VMEM((ways, SUMROWS, width), f32),
        gathered,
        gathered,
        pltpu.VMEM((tokens, HD), f32),
        head_block,
        head_block,
        head_block,
        flat,
        flat,
        kv_block,
        kv_block,
        kv_block,
        kv_block,
        wide,
        gathered,
        gathered,
        wide,
        gathered,
        gathered,
        pltpu.VMEM((tokens, 2 * HD), grad_kv_type),
        pltpu.VMEM((ways, tokens, 2 * HD), grad_kv_type),
        pltpu.VMEM((tokens, 2 * KVH * HD), f32),
        pltpu.VMEM((tokens, 2 * KVH * HD), bf16),
        pltpu.VMEM((tokens, width), bf16),
        pltpu.VMEM((tokens, width), bf16),
        pltpu.VMEM((tokens, width), bf16),
        pltpu.VMEM((tokens, width), f32),
        pltpu.VMEM((ways, SUMROWS, tokens), f32),
        pltpu.SemaphoreType.DMA((3,)),
        pltpu.SemaphoreType.DMA((copies,)),
        pltpu.SemaphoreType.DMA((copies,)),
    ]
    macs = 5 * tokens * model * local + 3 * tokens * width * 2 * KVH * HD
    next_input, received, input_grad = pl.pallas_call(
        functools.partial(layer_kernel, ways, sections),
        out_shape=(block, block, block),
        in_specs=[pl.BlockSpec(memory_space=pltpu.SMEM)]
        + [vmem] * 6
        + [pl.BlockSpec(memory_space=pl.ANY)] * 3,
        out_specs=(vmem, vmem, vmem),
        scratch_shapes=scratch,
        cost_estimate=pl.CostEstimate(
            flops=2 * macs,
            bytes_accessed=2 * (2 * model * local + width * 2 * KVH * HD + 8 * tokens * width),
            transcendentals=2 * heads_here * tokens * tokens,
        ),
        compiler_params=pltpu.CompilerParams(
            collective_id=0, has_side_effects=True, vmem_limit_bytes=56 * 1024 * 1024
        ),
        name="attention_layer",
    )(
        reload_slot,
        section_input[0],
        stash_pool[0],
        cotangent[0],
        norm_gain,
        jnp.asarray(cos_table),
        jnp.asarray(sin_table),
        query_weight[0],
        kv_weight[0],
        out_weight[0],
    )
    return (next_input[None], received[None], input_grad[None])


def solution(mesh):
    return jax.shard_map(
        functools.partial(per_device, mesh.shape["tensor"], mesh.shape["section"]),
        mesh=mesh,
        in_specs=(
            P("section", "dp", "tensor"),
            P("section", None, "dp", "tensor"),
            P("section"),
            P("section", "dp", "tensor"),
            P("section", "tensor"),
            P("section", None, "tensor"),
            P("section", "tensor", None),
            P("section", "tensor", None),
        ),
        out_specs=(
            P("section", "dp", "tensor"),
            P("section", "dp", "tensor"),
            P("section", "dp", "tensor"),
        ),
        check_vma=False,
    )
```

time: 385 us -> 87.3 us (0.23)
  waiting for transfers between devices: 225 us -> 0 us
  Pallas kernels: 0 us -> 80.7 us
  blocking collectives: 52.9 us -> 0 us
  matrix products: 46.5 us -> 0 us
  local copies, waits for them, and re-layouts: 23.2 us -> 5.01 us
  between operations: 15.3 us -> 1.29 us
  starting transfers between devices: 10.8 us -> 0 us
  other arithmetic: 10.7 us -> 0 us
    psum x3 -> x0, waiting for transfers between devices: 126 us -> none  [the longest x2 76.8 us: tensor_total(): return lax.psum(partial_value, 'tensor')]
    pallas_call x0 -> x1, Pallas kernels: none -> 80.7 us  [per_device(): pl.pallas_call(functools.partial(layer_kernel, ways, sections), out_shape...]
    all_gather x3 -> x0, waiting for transfers between devices: 74 us -> none  [gather_features(): return lax.all_gather(local_cols, 'tensor', axis=1, tiled=True)]
    psum x3 -> x0, blocking collectives: 52.9 us -> none  [the longest x1 34.9 us: tensor_total(): return lax.psum(partial_value, 'tensor')]
    dot_general x13 -> x0, matrix products: 42.5 us -> none  [the longest x3 15.9 us: contract_last(): lax.dot_general(left_side, right_side, (((1,), (1,)), ((), ())), preferre...]
    ppermute x4 -> x0, waiting for transfers between devices: 23.1 us -> none  [the longest x2 17.6 us: from_partner(): return lax.ppermute(value, axis, pairs)]
    dot_general x1 -> x0, local copies, waits for them, and re-layouts: 11.2 us -> none  [local_heads(): jnp.dot(gathered, query_w, preferred_element_type=jnp.float32)]
    ppermute x4 -> x0, starting transfers between devices: 10.5 us -> none  [the longest x2 5.84 us: from_partner(): return lax.ppermute(value, axis, pairs)]
  transfers between devices with their start and end apart: 11 -> 0, of which waited for: 9 -> 0; matrix products, arithmetic and copies ran while one was open for 8% -> 0% of each run, Pallas kernels for 0% -> 0%
where the time goes in v1:
time: 87.3 us; the launch traced here: 87 us
  Pallas kernels  80.7 us (92%)
  local copies, waits for them, and re-layouts  5.01 us (6%)
  between operations  1.29 us (1%)
    pallas_call x1, Pallas kernels, per_device(): pl.pallas_call(functools.partial(layer_kernel, ways, sections), out_shape...  80.7 us
    unnamed x3, local copies, waits for them, and re-layouts  5.01 us

profile of v1, /device:TPU:0, one launch (start us, length us, event | category | flops | bytes accessed | tf_op | source)
XLA Modules:
  0.0 87.0 jit_solution(16502235174480548235)
XLA Ops:
  1.3 80.7 %attention_layer.1 = (bf16[128,1024]{1,0:T(8,128)(2,1)}, bf16[128,1024]{1,0:T(8,128)(2,1)}, bf16[128,1024]{1,0:T(8,128)(2,1)}) custom-call(s32[1]{0:T(128)S(6)} %copy.16.slot_ref, bf16[128,1024]{1,0:T(8,128)(2,1)} %bitcast.16, bf16[2,128,1024]{2,1,0:T(8,128)(2,1)} %bitcast.15, bf16[128,1024]{1,0:T(8,128)(2,1)} %bitcast.17, f32[1,1024]{1,0:T(1,128)} %gain_ref.1, ...), custom_call_target="tpu_custom_call" | custom-call | flops 6174015488 | bytes 20971520 | tf_op jit(solution)/shard_map/attention_layer/pallas_call | solution.py:575
  82.0 1.7 %copy.17 = bf16[1,128,1024]{2,1,0:T(8,128)(2,1)} copy(bf16[1,128,1024]{2,1,0:T(8,128)(2,1)} %bitcast.11) | data formatting | bytes 524288
  83.7 1.7 %copy.18 = bf16[1,128,1024]{2,1,0:T(8,128)(2,1)} copy(bf16[1,128,1024]{2,1,0:T(8,128)(2,1)} %bitcast.10) | data formatting | bytes 524288
  85.3 1.7 %copy.19 = bf16[1,128,1024]{2,1,0:T(8,128)(2,1)} copy(bf16[1,128,1024]{2,1,0:T(8,128)(2,1)} %bitcast.9) | data formatting | bytes 524288

commit v2 on v1

--- a/solution.py
+++ b/solution.py
@@ -14,7 +14,7 @@
 PAIR = 2
 TILE = 256
 SUMROWS = 8
-ZCHUNKS = 4
+PIECES = 2
 
 norm_eps = 1e-05
 f32 = jnp.float32
@@ -75,13 +75,13 @@
     qw,
     kvw,
     ow,
-    xg,
-    bg,
     cg,
-    gg,
     fn,
     bn,
-    fact,
+    back,
+    c_acc,
+    f_acc,
+    b_acc,
     qf,
     qb,
     go,
@@ -97,15 +97,15 @@
     gq_p,
     gq_s,
     gq_r,
-    gk_s,
     gk_r,
     gk_acc,
     gk_full,
     trav,
     lo,
     gl,
-    scaled,
-    msum,
+    f_sum,
+    b_sum,
+    m_sum,
     wsem,
     ssem,
     rsem,
@@ -128,12 +128,15 @@
     relay = ways == 4
     per_group = ways // KVH
     groups = [lax.div(p, per_group) for p in peers]
-
-    loads = [
+    pieces = PIECES if width % (PIECES * TILE) == 0 else 1
+    piece_width = width // pieces
+    piece_cols = [pl.ds(p * piece_width, piece_width) for p in range(pieces)]
+
+    load_ow, load_kvw, load_qw = [
         pltpu.make_async_copy(a, b, wsem.at[i])
-        for i, (a, b) in enumerate(((kvw_hbm, kvw), (qw_hbm, qw), (ow_hbm, ow)))
+        for i, (a, b) in enumerate(((ow_hbm, ow), (kvw_hbm, kvw), (qw_hbm, qw)))
     ]
-    for load in loads:
+    for load in (load_ow, load_kvw, load_qw):
         load.start()
 
     used = []
@@ -185,10 +188,42 @@
     def _():
         trav[...] = stash_ref[slot_ref[0]]
 
-    xg[0] = x_ref[...]
     cg[0] = cot_ref[...]
-    gg[0] = jnp.broadcast_to(gain_ref[...], gg.shape[1:])
-
+
+    eye = lax.broadcasted_iota(jnp.int32, (tokens, tokens), 0) == lax.broadcasted_iota(
+        jnp.int32, (tokens, tokens), 1
+    )
+    step = 32
+
+    def squares(rows_ref):
+        sums = []
+        for r in range(0, tokens, step):
+            v = rows_ref[r : r + step, :].astype(f32)
+            sums.append(jnp.sum(v * v, axis=-1, keepdims=True))
+        return jnp.concatenate(sums, axis=0)
+
+    def sum_put(column, buf):
+        as_row = jnp.sum(jnp.where(eye, column, 0.0), axis=0, keepdims=True)
+        buf[0] = jnp.broadcast_to(as_row, (SUMROWS, tokens))
+
+    def sum_send(buf):
+        return [to_peer(k, buf.at[0], buf.at[k]) for k in range(1, ways)]
+
+    def sum_total(copies, buf):
+        finish(copies)
+        total = buf[0, 0:1, :]
+        for k in range(1, ways):
+            total = total + buf[k, 0:1, :]
+        return jnp.sum(jnp.where(eye, total, 0.0), axis=1, keepdims=True)
+
+    def normalize(rows_ref, out, total):
+        factor = lax.rsqrt(total / model + norm_eps)
+        for r in range(0, tokens, step):
+            v = rows_ref[r : r + step, :].astype(f32)
+            out[0, r : r + step, :] = (v * factor[r : r + step] * gain_ref[...]).astype(bf16)
+        return factor
+
+    sum_put(squares(x_ref), f_sum)
     pl.semaphore_wait(barrier, ways + jnp.minimum(sec, 1) + jnp.minimum(sections - 1 - sec, 1))
 
     def gather_start(buf):
@@ -198,7 +233,8 @@
 
     def gather_pass_on(buf, copies):
         if not relay:
-            return copies
+            finish(copies)
+            return []
         copies[0].wait_recv()
         first = to_peer(2, buf.at[1, upper], buf.at[3, upper])
         copies[1].wait_recv()
@@ -211,29 +247,31 @@
 
     order = (3, 1, 2, 0) if relay else tuple(range(1, ways)) + (0,)
 
-    def reduce_send(k, stage, land):
+    def reduce_send(k, stage, land, cols):
         if k == 0:
             return []
         if not relay:
-            return [to_peer(k, stage.at[k], land.at[k])]
+            return [to_peer(k, stage.at[k, :, cols], land.at[k, :, cols])]
         if k == 3:
             return [
-                to_peer(1, stage.at[3, upper], land.at[2, upper]),
-                to_peer(2, stage.at[3, lower], land.at[1, lower]),
+                to_peer(1, stage.at[3, upper, cols], land.at[2, upper, cols]),
+                to_peer(2, stage.at[3, lower, cols], land.at[1, lower, cols]),
             ]
         if k == 1:
-            return [to_peer(1, stage.at[1, upper], land.at[0, upper])]
-        return [to_peer(2, stage.at[2, lower], land.at[0, lower])]
-
-    def reduce_pass_on(copies, part, stage, land):
+            return [to_peer(1, stage.at[1, upper, cols], land.at[0, upper, cols])]
+        return [to_peer(2, stage.at[2, lower, cols], land.at[0, lower, cols])]
+
+    def reduce_pass_on(copies, part, stage, land, cols):
         if not relay:
             return copies
         copies[0].wait_recv()
-        stage[2, upper] = (part[2, upper] + land[2, upper].astype(f32)).astype(stage.dtype)
-        first = to_peer(2, stage.at[2, upper], land.at[3, upper])
+        summed = part[2, upper, cols] + land[2, upper, cols].astype(f32)
+        stage[2, upper, cols] = summed.astype(stage.dtype)
+        first = to_peer(2, stage.at[2, upper, cols], land.at[3, upper, cols])
         copies[1].wait_recv()
-        stage[1, lower] = (part[1, lower] + land[1, lower].astype(f32)).astype(stage.dtype)
-        second = to_peer(1, stage.at[1, lower], land.at[3, lower])
+        summed = part[1, lower, cols] + land[1, lower, cols].astype(f32)
+        stage[1, lower, cols] = summed.astype(stage.dtype)
+        second = to_peer(1, stage.at[1, lower, cols], land.at[3, lower, cols])
         return copies[2:] + [first, second]
 
     def reduced(part, land, rows, cols):
@@ -242,24 +280,8 @@
             total = total + land[k, rows, cols].astype(f32)
         return total
 
-    def normalize(raw, out, keep):
-        step = 16
-
-        def body(i, carry):
-            rows = pl.ds(pl.multiple_of(i * step, step), step)
-            total = jnp.zeros((step, 1), f32)
-            for k in range(ways):
-                v = raw[k, rows, :].astype(f32)
-                total = total + jnp.sum(v * v, axis=-1, keepdims=True)
-            factor = lax.rsqrt(total / model + norm_eps)
-            for k in range(ways):
-                v = raw[k, rows, :].astype(f32)
-                out[k, rows, :] = (v * factor * gg[k, 0:1, :]).astype(bf16)
-            if keep:
-                fact[rows, :] = jnp.broadcast_to(factor, (step, HD))
-            return carry
-
-        lax.fori_loop(0, tokens // step, body, 0)
+    kv_cols = pl.ds(0, 2 * HD)
+    everything = pl.ds(0, tokens)
 
     def kv_terms(normed, part, land):
         copies = []
@@ -268,7 +290,7 @@
             value_cols = pl.ds(pl.multiple_of((KVH + groups[k]) * HD, HD), HD)
             part[k, :, 0:HD] = dot_nn(normed[0], kvw[:, key_cols])
             part[k, :, HD : 2 * HD] = dot_nn(normed[0], kvw[:, value_cols])
-            copies += reduce_send(k, part, land)
+            copies += reduce_send(k, part, land, kv_cols)
         return copies
 
     def rotate(u):
@@ -280,24 +302,42 @@
     per_tile = TILE // HD
     scale = HD ** (-0.5)
 
-    def queries(normed, out):
+    def accumulate(ks, buf, weight_tile, acc, out=None, finished=None):
         def body(n, carry):
             cols = pl.ds(pl.multiple_of(n * TILE, TILE), TILE)
-            acc = dot_nn(normed[0], qw[rows_of[0], cols])
-            for k in range(1, ways):
-                acc = acc + dot_nn(normed[k], qw[rows_of[k], cols])
-            for j in range(per_tile):
-                head = acc[:, j * HD : (j + 1) * HD]
-                out[n * per_tile + j] = (rotate(head) * scale).astype(bf16)
+            total = weight_tile(buf, ks[0], cols)
+            for k in ks[1:]:
+                total = total + weight_tile(buf, k, cols)
+            if ks[0] != 0:
+                total = total + acc[:, cols]
+            acc[:, cols] = total
+            if out is not None:
+                for j in range(per_tile):
+                    head = total[:, j * HD : (j + 1) * HD]
+                    out[n * per_tile + j] = finished(head).astype(bf16)
             return carry
 
         lax.fori_loop(0, heads_here // per_tile, body, 0)
 
+    def query_block(buf, k, cols):
+        return dot_nn(buf[k], qw[rows_of[k], cols])
+
+    def cot_block(buf, k, rows):
+        return dot_nt(buf[k], ow[rows, rows_of[k]])
+
+    def turned_query(head):
+        return rotate(head) * scale
+
+    def plain(head):
+        return head
+
+    near = [1, 2] if relay else list(range(1, ways // 2))
+    far = [3] if relay else list(range(ways // 2, ways))
+
     def key_value(part, land):
-        everything = pl.ds(0, tokens)
-        key = rotate(reduced(part, land, everything, pl.ds(0, HD))).astype(bf16)
-        value = reduced(part, land, everything, pl.ds(HD, HD)).astype(bf16)
-        return key, value
+        key_wide = reduced(part, land, everything, pl.ds(0, HD))
+        value_wide = reduced(part, land, everything, pl.ds(HD, HD))
+        return rotate(key_wide).astype(bf16), value_wide.astype(bf16), key_wide, value_wide
 
     span = PAIR * tokens
     position = lax.rem(lax.broadcasted_iota(jnp.int32, (span, tokens), 0), tokens)
@@ -310,19 +350,23 @@
 
     def project(source, weight_tile, part, stage, land):
         copies = []
-        for k in order:
-
-            def body(n, carry, k=k):
-                cols = pl.ds(pl.multiple_of(n * TILE, TILE), TILE)
-                value = weight_tile(source, k, n)
-                if not (relay and k == 3):
-                    part[k, :, cols] = value
-                if k:
-                    stage[k, :, cols] = value.astype(bf16)
-                return carry
-
-            lax.fori_loop(0, width // TILE, body, 0)
-            copies += reduce_send(k, stage, land)
+        tiles = piece_width // TILE
+        for p in range(pieces):
+            copies.append([])
+            for k in order:
+
+                def body(n, carry, k=k, p=p):
+                    n = p * tiles + n
+                    cols = pl.ds(pl.multiple_of(n * TILE, TILE), TILE)
+                    value = weight_tile(source, k, n)
+                    if not (relay and k == 3):
+                        part[k, :, cols] = value
+                    if k:
+                        stage[k, :, cols] = value.astype(bf16)
+                    return carry
+
+                lax.fori_loop(0, tiles, body, 0)
+                copies[p] += reduce_send(k, stage, land, piece_cols[p])
         return copies
 
     def out_tile(source, k, n):
@@ -334,33 +378,46 @@
         return dot_nt(source[...], qw[rows, :])
 
     travel_copy = send(trav, travel_ref, "section", mirror)
-    gain_copies = [to_peer(k, gg.at[0], gg.at[k]) for k in range(1, ways)]
-    x_copies = gather_start(xg)
-    x_copies = gather_pass_on(xg, x_copies)
+    f_sums = sum_send(f_sum)
+    c_copies = gather_start(cg)
+
+    load_ow.wait()
+    accumulate([0], cg, cot_block, c_acc)
+    normalize(x_ref, fn, sum_total(f_sums, f_sum))
+    load_kvw.wait()
+    kvf = kv_terms(fn, kvf_p, kvf_r)
+    c_copies = gather_pass_on(cg, c_copies)
+    x_copies = gather_start(fn)
+    accumulate(near, cg, cot_block, c_acc)
+    kvf = reduce_pass_on(kvf, kvf_p, kvf_p, kvf_r, kv_cols)
+    load_qw.wait()
+    accumulate([0], fn, query_block, f_acc)
 
     travel_copy.wait_recv()
 
     @pl.when(early)
     def _():
-        bg[0] = travel_ref[...]
+        back[...] = travel_ref[...]
 
     @pl.when(jnp.logical_not(early))
     def _():
-        bg[0] = x_ref[...]
-
-    b_copies = gather_start(bg)
-    finish(gain_copies)
+        back[...] = x_ref[...]
+
+    sum_put(squares(back), b_sum)
+    b_sums = sum_send(b_sum)
+    finish(c_copies)
+    accumulate(far, cg, cot_block, c_acc, go, plain)
+    factor = normalize(back, bn, sum_total(b_sums, b_sum))
+    kvb = kv_terms(bn, kvb_p, kvb_r)
+    x_copies = gather_pass_on(fn, x_copies)
+    b_copies = gather_start(bn)
+    accumulate(near, fn, query_block, f_acc)
+    kvb = reduce_pass_on(kvb, kvb_p, kvb_p, kvb_r, kv_cols)
+    accumulate([0], bn, query_block, b_acc)
+    finish(kvf)
+    key, value, _, _ = key_value(kvf_p, kvf_r)
     finish(x_copies)
-    normalize(xg, fn, False)
-    loads[0].wait()
-    kvf = kv_terms(fn, kvf_p, kvf_r)
-    loads[1].wait()
-    queries(fn, qf)
-    kvf = reduce_pass_on(kvf, kvf_p, kvf_p, kvf_r)
-    b_copies = gather_pass_on(bg, b_copies)
-    c_copies = gather_start(cg)
-    finish(kvf)
-    key, value = key_value(kvf_p, kvf_r)
+    accumulate(far, fn, query_block, f_acc, qf, turned_query)
     for i in range(heads_here // PAIR):
         q = qf[PAIR * i : PAIR * (i + 1)].reshape(span, HD)
         weights = probabilities(q, key).astype(bf16)
@@ -369,31 +426,19 @@
             head = PAIR * i + j
             att[:, head * HD : (head + 1) * HD] = result[j * tokens : (j + 1) * tokens]
 
+    b_copies = gather_pass_on(bn, b_copies)
+    outs = project(att, out_tile, out_p, out_s, out_r)
+    accumulate(near, bn, query_block, b_acc)
+    for p in range(pieces):
+        outs[p] = reduce_pass_on(outs[p], out_p, out_s, out_r, piece_cols[p])
     finish(b_copies)
-    normalize(bg, bn, True)
-    kvb = kv_terms(bn, kvb_p, kvb_r)
-    loads[2].wait()
-    outs = project(att, out_tile, out_p, out_s, out_r)
-    queries(bn, qb)
-    kvb = reduce_pass_on(kvb, kvb_p, kvb_p, kvb_r)
-    c_copies = gather_pass_on(cg, c_copies)
-    outs = reduce_pass_on(outs, out_p, out_s, out_r)
-    finish(c_copies)
-
-    def cot_body(n, carry):
-        rows = pl.ds(pl.multiple_of(n * TILE, TILE), TILE)
-        acc = dot_nt(cg[0], ow[rows, rows_of[0]])
-        for k in range(1, ways):
-            acc = acc + dot_nt(cg[k], ow[rows, rows_of[k]])
-        for j in range(per_tile):
-            go[n * per_tile + j] = acc[:, j * HD : (j + 1) * HD].astype(bf16)
-        return carry
-
-    lax.fori_loop(0, heads_here // per_tile, cot_body, 0)
+    accumulate(far, bn, query_block, b_acc, qb, turned_query)
+
     finish(kvb)
-    key, value = key_value(kvb_p, kvb_r)
+    key, value, key_wide, value_wide = key_value(kvb_p, kvb_r)
     grad_key = jnp.zeros((tokens, HD), f32)
     grad_value = jnp.zeros((tokens, HD), f32)
+    mixed = jnp.zeros((tokens, HD), f32)
     for i in range(heads_here // PAIR):
         q = qb[PAIR * i : PAIR * (i + 1)].reshape(span, HD)
         g = go[PAIR * i : PAIR * (i + 1)].reshape(span, HD)
@@ -404,27 +449,35 @@
         grad_q = dot_nn(grad_scores, key)
         for j in range(PAIR):
             head = PAIR * i + j
-            turned = unrotate(grad_q[j * tokens : (j + 1) * tokens]) * scale
-            gqb[:, head * HD : (head + 1) * HD] = turned.astype(bf16)
+            turned = (unrotate(grad_q[j * tokens : (j + 1) * tokens]) * scale).astype(bf16)
+            gqb[:, head * HD : (head + 1) * HD] = turned
+            mixed = mixed + turned.astype(f32) * b_acc[:, head * HD : (head + 1) * HD]
         grad_key = grad_key + dot_tn(grad_scores, q)
         grad_value = grad_value + dot_tn(probs.astype(bf16), g)
-    gk_r[0, :, 0:HD] = unrotate(grad_key).astype(gk_r.dtype)
-    gk_r[0, :, HD : 2 * HD] = grad_value.astype(gk_r.dtype)
+    grad_key = unrotate(grad_key).astype(gk_r.dtype)
+    grad_value = grad_value.astype(gk_r.dtype)
+    gk_r[0, :, 0:HD] = grad_key
+    gk_r[0, :, HD : 2 * HD] = grad_value
     gk_copies = [to_peer(k, gk_r.at[0], gk_r.at[k]) for k in range(1, ways)]
+    mixed = mixed + grad_key.astype(f32) * key_wide + grad_value.astype(f32) * value_wide
+    sum_put(jnp.sum(mixed, axis=-1, keepdims=True), m_sum)
+    m_sums = sum_send(m_sum)
     grads = project(gqb, query_tile, gq_p, gq_s, gq_r)
 
-    finish(outs)
-    chunk = tokens // ZCHUNKS
     next_copies = []
-    for c in range(ZCHUNKS):
-        rows = pl.ds(c * chunk, chunk)
-        total = reduced(out_p, out_r, rows, pl.ds(0, width))
-        lo[rows, :] = (x_ref[rows, :].astype(f32) + total).astype(bf16)
-        copy = send(lo.at[rows], next_ref.at[rows], "section", nxt, start=False)
-        pl.when(has_next)(copy.start)
-        next_copies.append(copy)
-
-    grads = reduce_pass_on(grads, gq_p, gq_s, gq_r)
+    grad_copies = []
+    row_chunks = (upper, lower)
+
+    for p in range(pieces):
+        finish(outs[p])
+        for rows in row_chunks:
+            cols = piece_cols[p]
+            total = reduced(out_p, out_r, rows, cols)
+            lo[rows, cols] = (x_ref[rows, cols].astype(f32) + total).astype(bf16)
+            copy = send(lo.at[rows, cols], next_ref.at[rows, cols], "section", nxt, start=False)
+            pl.when(has_next)(copy.start)
+            next_copies.append(copy)
+        grads[p] = reduce_pass_on(grads[p], gq_p, gq_s, gq_r, piece_cols[p])
 
     finish(gk_copies)
     if per_group == 1:
@@ -444,35 +497,20 @@
     for n in range(width // TILE):
         cols = pl.ds(n * TILE, TILE)
         gq_p[0, :, cols] += dot_nt(gk_full[...], kvw[cols, :])
-
-    finish(grads)
-    row_sum = jnp.zeros((tokens, 1), f32)
-    for n in range(width // TILE):
-        cols = pl.ds(n * TILE, TILE)
-        part = reduced(gq_p, gq_r, pl.ds(0, tokens), cols) * gain_ref[:, cols]
-        scaled[:, cols] = part
-        row_sum = row_sum + jnp.sum(part * bg[0, :, cols].astype(f32), axis=-1, keepdims=True)
-    eye = lax.broadcasted_iota(jnp.int32, (tokens, tokens), 0) == lax.broadcasted_iota(
-        jnp.int32, (tokens, tokens), 1
-    )
-    as_row = jnp.sum(jnp.where(eye, row_sum, 0.0), axis=0, keepdims=True)
-    msum[0] = jnp.broadcast_to(as_row, (SUMROWS, tokens))
-    finish([to_peer(k, msum.at[0], msum.at[k]) for k in range(1, ways)])
-    total = msum[0, 0:1, :]
-    for k in range(1, ways):
-        total = total + msum[k, 0:1, :]
-    mean = jnp.sum(jnp.where(eye, total, 0.0), axis=1, keepdims=True) / model
-    grad_copies = []
-    for c in range(ZCHUNKS):
-        rows = pl.ds(c * chunk, chunk)
-        factor = fact[rows, 0:1]
-        back = bg[0, rows, :].astype(f32)
-        cube = factor * factor * factor * mean[c * chunk : (c + 1) * chunk]
-        grad_rows = factor * scaled[rows, :] - back * cube
-        gl[rows, :] = (cot_ref[rows, :].astype(f32) + grad_rows).astype(bf16)
-        copy = send(gl.at[rows], igrad_ref.at[rows], "section", prev, start=False)
-        pl.when(has_prev)(copy.start)
-        grad_copies.append(copy)
+    square_mean = factor * factor * (sum_total(m_sums, m_sum) / model)
+
+    for p in range(pieces):
+        finish(grads[p])
+        cols = piece_cols[p]
+        for c, rows in enumerate(row_chunks):
+            here = slice(c * half, (c + 1) * half)
+            g = reduced(gq_p, gq_r, rows, cols) * gain_ref[:, cols]
+            b = back[rows, cols].astype(f32)
+            grad_rows = factor[here] * g - b * square_mean[here]
+            gl[rows, cols] = (cot_ref[rows, cols].astype(f32) + grad_rows).astype(bf16)
+            copy = send(gl.at[rows, cols], igrad_ref.at[rows, cols], "section", prev, start=False)
+            pl.when(has_prev)(copy.start)
+            grad_copies.append(copy)
 
     @pl.when(jnp.logical_not(has_prev))
     def _():
@@ -500,10 +538,21 @@
             copy.wait_send()
 
 
+def hand_on(a, b, c, a_out, b_out, c_out, sem):
+    copies = [
+        pltpu.make_async_copy(src, dst, sem.at[i])
+        for i, (src, dst) in enumerate(((a, a_out), (b, b_out), (c, c_out)))
+    ]
+    for copy in copies:
+        copy.start()
+    for copy in copies:
+        copy.wait()
+
+
 def copies_needed(ways):
     if ways == 4:
-        return 1 + 3 + 3 * 4 + 4 * 6 + 3 + 3 + 2 * ZCHUNKS
-    return 1 + (ways - 1) * 10 + 2 * ZCHUNKS
+        return 1 + 9 + 3 * 4 + 2 * 6 + 2 * PIECES * 6 + 3 + 4 * PIECES
+    return 1 + (ways - 1) * (3 + 3 + 2 + 2 * PIECES + 1) + 4 * PIECES
 
 
 def per_device(
@@ -532,6 +581,9 @@
     kv_block = pltpu.VMEM((ways, tokens, 2 * HD), f32)
     head_block = pltpu.VMEM((heads_here, tokens, HD), bf16)
     flat = pltpu.VMEM((tokens, local), bf16)
+    sums = pltpu.VMEM((ways, SUMROWS, tokens), f32)
+    local_wide = pltpu.VMEM((tokens, local), f32)
+    flat_block = pltpu.VMEM((tokens, width), bf16)
     scratch = [
         pltpu.VMEM((model, local), bf16),
         pltpu.VMEM((width, 2 * KVH * HD), bf16),
@@ -539,10 +591,10 @@
         gathered,
         gathered,
         gathered,
-        pltpu.VMEM((ways, SUMROWS, width), f32),
-        gathered,
-        gathered,
-        pltpu.VMEM((tokens, HD), f32),
+        flat_block,
+        local_wide,
+        local_wide,
+        local_wide,
         head_block,
         head_block,
         head_block,
@@ -558,15 +610,15 @@
         wide,
         gathered,
         gathered,
-        pltpu.VMEM((tokens, 2 * HD), grad_kv_type),
         pltpu.VMEM((ways, tokens, 2 * HD), grad_kv_type),
         pltpu.VMEM((tokens, 2 * KVH * HD), f32),
         pltpu.VMEM((tokens, 2 * KVH * HD), bf16),
-        pltpu.VMEM((tokens, width), bf16),
-        pltpu.VMEM((tokens, width), bf16),
-        pltpu.VMEM((tokens, width), bf16),
-        pltpu.VMEM((tokens, width), f32),
-        pltpu.VMEM((ways, SUMROWS, tokens), f32),
+        flat_block,
+        flat_block,
+        flat_block,
+        sums,
+        sums,
+        sums,
         pltpu.SemaphoreType.DMA((3,)),
         pltpu.SemaphoreType.DMA((copies,)),
         pltpu.SemaphoreType.DMA((copies,)),
@@ -601,6 +653,15 @@
         kv_weight[0],
         out_weight[0],
     )
+    anywhere = pl.BlockSpec(memory_space=pl.ANY)
+    next_input, received, input_grad = pl.pallas_call(
+        hand_on,
+        out_shape=(block, block, block),
+        in_specs=[anywhere] * 3,
+        out_specs=(anywhere,) * 3,
+        scratch_shapes=[pltpu.SemaphoreType.DMA((3,))],
+        name="results",
+    )(next_input, received, input_grad)
     return (next_input[None], received[None], input_grad[None])
 
 

time: 87.3 us -> 96.2 us (1.10)
  Pallas kernels: 80.7 us -> 94.8 us
  local copies, waits for them, and re-layouts: 5.01 us -> 0 us
    pallas_call x0 -> x1, Pallas kernels: none -> 25 us  [per_device(): pl.pallas_call(hand_on, out_shape=(block, block, block), in_specs=[anywhe...]
    pallas_call x1, Pallas kernels: 80.7 us -> 69.9 us  [per_device(): pl.pallas_call(functools.partial(layer_kernel, ways, sections), out_shape...]
    unnamed x3 -> x0, local copies, waits for them, and re-layouts: 5.01 us -> none
where the time goes in v2:
time: 96.2 us; the launch traced here: 96.1 us
  Pallas kernels  94.8 us (99%)
  between operations  1.29 us (1%)
    pallas_call x1, Pallas kernels, per_device(): pl.pallas_call(functools.partial(layer_kernel, ways, sections), out_shape...  69.9 us
    pallas_call x1, Pallas kernels, per_device(): pl.pallas_call(hand_on, out_shape=(block, block, block), in_specs=[anywhe...  25 us

profile of v2, /device:TPU:0, one launch (start us, length us, event | category | flops | bytes accessed | tf_op | source)
XLA Modules:
  0.0 96.1 jit_solution(6881503537950321049)
XLA Ops:
  1.3 69.9 %attention_layer.1 = (bf16[128,1024]{1,0:T(8,128)(2,1)}, bf16[128,1024]{1,0:T(8,128)(2,1)}, bf16[128,1024]{1,0:T(8,128)(2,1)}) custom-call(s32[1]{0:T(128)S(6)} %copy.13.slot_ref, bf16[128,1024]{1,0:T(8,128)(2,1)} %bitcast.13, bf16[2,128,1024]{2,1,0:T(8,128)(2,1)} %bitcast.12, bf16[128,1024]{1,0:T(8,128)(2,1)} %bitcast.14, f32[1,1024]{1,0:T(1,128)} %gain_ref.1, ...), custom_call_target="tpu_custom_call" | custom-call | flops 6174015488 | bytes 20971520 | tf_op jit(solution)/shard_map/attention_layer/pallas_call | solution.py:627
  71.1 25.0 %results.1 = (bf16[128,1024]{1,0:T(8,128)(2,1)}, bf16[128,1024]{1,0:T(8,128)(2,1)}, bf16[128,1024]{1,0:T(8,128)(2,1)}) custom-call(bf16[128,1024]{1,0:T(8,128)(2,1)} %get-tuple-element.9.a, bf16[128,1024]{1,0:T(8,128)(2,1)} %get-tuple-element.10.b, bf16[128,1024]{1,0:T(8,128)(2,1)} %get-tuple-element.11.c), custom_call_target="tpu_custom_call" | custom-call | tf_op jit(solution)/shard_map/results/pallas_call | solution.py:657

commit v3 on v2

--- a/solution.py
+++ b/solution.py
@@ -132,11 +132,11 @@
     piece_width = width // pieces
     piece_cols = [pl.ds(p * piece_width, piece_width) for p in range(pieces)]
 
-    load_ow, load_kvw, load_qw = [
+    load_kvw, load_qw, load_ow = [
         pltpu.make_async_copy(a, b, wsem.at[i])
-        for i, (a, b) in enumerate(((ow_hbm, ow), (kvw_hbm, kvw), (qw_hbm, qw)))
+        for i, (a, b) in enumerate(((kvw_hbm, kvw), (qw_hbm, qw), (ow_hbm, ow)))
     ]
-    for load in (load_ow, load_kvw, load_qw):
+    for load in (load_kvw, load_qw, load_ow):
         load.start()
 
     used = []
@@ -226,10 +226,21 @@
     sum_put(squares(x_ref), f_sum)
     pl.semaphore_wait(barrier, ways + jnp.minimum(sec, 1) + jnp.minimum(sections - 1 - sec, 1))
 
-    def gather_start(buf):
+    def gather_first(buf):
         if relay:
-            return [to_peer(k, buf.at[0], buf.at[k]) for k in (1, 2)]
+            return [
+                to_peer(1, buf.at[0, upper], buf.at[1, upper]),
+                to_peer(2, buf.at[0, lower], buf.at[2, lower]),
+            ]
         return [to_peer(k, buf.at[0], buf.at[k]) for k in range(1, ways)]
+
+    def gather_second(buf):
+        if relay:
+            return [
+                to_peer(1, buf.at[0, lower], buf.at[1, lower]),
+                to_peer(2, buf.at[0, upper], buf.at[2, upper]),
+            ]
+        return []
 
     def gather_pass_on(buf, copies):
         if not relay:
@@ -280,7 +291,11 @@
             total = total + land[k, rows, cols].astype(f32)
         return total
 
+    def tile_loop(count, body):
+        lax.fori_loop(0, count, body, 0, unroll=2 if count % 2 == 0 else 1)
+
     kv_cols = pl.ds(0, 2 * HD)
+    all_cols = pl.ds(0, width)
     everything = pl.ds(0, tokens)
 
     def kv_terms(normed, part, land):
@@ -317,7 +332,7 @@
                     out[n * per_tile + j] = finished(head).astype(bf16)
             return carry
 
-        lax.fori_loop(0, heads_here // per_tile, body, 0)
+        tile_loop(heads_here // per_tile, body)
 
     def query_block(buf, k, cols):
         return dot_nn(buf[k], qw[rows_of[k], cols])
@@ -348,26 +363,18 @@
         shifted = jnp.exp(scores - jnp.max(scores, axis=-1, keepdims=True))
         return shifted * (1.0 / jnp.sum(shifted, axis=-1, keepdims=True))
 
-    def project(source, weight_tile, part, stage, land):
-        copies = []
-        tiles = piece_width // TILE
-        for p in range(pieces):
-            copies.append([])
-            for k in order:
-
-                def body(n, carry, k=k, p=p):
-                    n = p * tiles + n
-                    cols = pl.ds(pl.multiple_of(n * TILE, TILE), TILE)
-                    value = weight_tile(source, k, n)
-                    if not (relay and k == 3):
-                        part[k, :, cols] = value
-                    if k:
-                        stage[k, :, cols] = value.astype(bf16)
-                    return carry
-
-                lax.fori_loop(0, tiles, body, 0)
-                copies[p] += reduce_send(k, stage, land, piece_cols[p])
-        return copies
+    def project(source, weight_tile, part, stage, k, first, count):
+        def body(n, carry):
+            n = first + n
+            cols = pl.ds(pl.multiple_of(n * TILE, TILE), TILE)
+            value = weight_tile(source, k, n)
+            if not (relay and k == 3):
+                part[k, :, cols] = value
+            if k:
+                stage[k, :, cols] = value.astype(bf16)
+            return carry
+
+        tile_loop(count, body)
 
     def out_tile(source, k, n):
         cols = pl.ds(pl.multiple_of(peers[k] * width + n * TILE, TILE), TILE)
@@ -379,19 +386,20 @@
 
     travel_copy = send(trav, travel_ref, "section", mirror)
     f_sums = sum_send(f_sum)
-    c_copies = gather_start(cg)
-
-    load_ow.wait()
-    accumulate([0], cg, cot_block, c_acc)
+    c_first = gather_first(cg)
     normalize(x_ref, fn, sum_total(f_sums, f_sum))
+    x_first = gather_first(fn)
+    x_second = gather_second(fn)
     load_kvw.wait()
     kvf = kv_terms(fn, kvf_p, kvf_r)
-    c_copies = gather_pass_on(cg, c_copies)
-    x_copies = gather_start(fn)
-    accumulate(near, cg, cot_block, c_acc)
-    kvf = reduce_pass_on(kvf, kvf_p, kvf_p, kvf_r, kv_cols)
     load_qw.wait()
     accumulate([0], fn, query_block, f_acc)
+    x_far = gather_pass_on(fn, x_first)
+    c_far = gather_pass_on(cg, c_first)
+    c_second = gather_second(cg)
+    kvf = reduce_pass_on(kvf, kvf_p, kvf_p, kvf_r, kv_cols)
+    finish(x_second)
+    accumulate(near, fn, query_block, f_acc)
 
     travel_copy.wait_recv()
 
@@ -405,19 +413,14 @@
 
     sum_put(squares(back), b_sum)
     b_sums = sum_send(b_sum)
-    finish(c_copies)
-    accumulate(far, cg, cot_block, c_acc, go, plain)
+    finish(x_far)
+    accumulate(far, fn, query_block, f_acc, qf, turned_query)
     factor = normalize(back, bn, sum_total(b_sums, b_sum))
+    b_first = gather_first(bn)
+    b_second = gather_second(bn)
     kvb = kv_terms(bn, kvb_p, kvb_r)
-    x_copies = gather_pass_on(fn, x_copies)
-    b_copies = gather_start(bn)
-    accumulate(near, fn, query_block, f_acc)
-    kvb = reduce_pass_on(kvb, kvb_p, kvb_p, kvb_r, kv_cols)
-    accumulate([0], bn, query_block, b_acc)
     finish(kvf)
     key, value, _, _ = key_value(kvf_p, kvf_r)
-    finish(x_copies)
-    accumulate(far, fn, query_block, f_acc, qf, turned_query)
     for i in range(heads_here // PAIR):
         q = qf[PAIR * i : PAIR * (i + 1)].reshape(span, HD)
         weights = probabilities(q, key).astype(bf16)
@@ -426,13 +429,21 @@
             head = PAIR * i + j
             att[:, head * HD : (head + 1) * HD] = result[j * tokens : (j + 1) * tokens]
 
-    b_copies = gather_pass_on(bn, b_copies)
-    outs = project(att, out_tile, out_p, out_s, out_r)
-    accumulate(near, bn, query_block, b_acc)
-    for p in range(pieces):
-        outs[p] = reduce_pass_on(outs[p], out_p, out_s, out_r, piece_cols[p])
-    finish(b_copies)
-    accumulate(far, bn, query_block, b_acc, qb, turned_query)
+    b_far = gather_pass_on(bn, b_first)
+    load_ow.wait()
+    outs = []
+    for k in order:
+        project(att, out_tile, out_p, out_s, k, 0, width // TILE)
+        if k == order[0]:
+            kvb = reduce_pass_on(kvb, kvb_p, kvb_p, kvb_r, kv_cols)
+        outs += reduce_send(k, out_s, out_r, all_cols)
+    finish(c_second)
+    finish(c_far)
+    accumulate(list(range(ways)), cg, cot_block, c_acc, go, plain)
+    outs = reduce_pass_on(outs, out_p, out_s, out_r, all_cols)
+    finish(b_second)
+    finish(b_far)
+    accumulate(list(range(ways)), bn, query_block, b_acc, qb, turned_query)
 
     finish(kvb)
     key, value, key_wide, value_wide = key_value(kvb_p, kvb_r)
@@ -462,21 +473,26 @@
     mixed = mixed + grad_key.astype(f32) * key_wide + grad_value.astype(f32) * value_wide
     sum_put(jnp.sum(mixed, axis=-1, keepdims=True), m_sum)
     m_sums = sum_send(m_sum)
-    grads = project(gqb, query_tile, gq_p, gq_s, gq_r)
+    grads = []
+    piece_tiles = piece_width // TILE
+    for p in range(pieces):
+        grads.append([])
+        for k in order:
+            project(gqb, query_tile, gq_p, gq_s, k, p * piece_tiles, piece_tiles)
+            grads[p] += reduce_send(k, gq_s, gq_r, piece_cols[p])
 
     next_copies = []
     grad_copies = []
     row_chunks = (upper, lower)
 
+    finish(outs)
+    for rows in row_chunks:
+        total = reduced(out_p, out_r, rows, all_cols)
+        lo[rows, :] = (x_ref[rows, :].astype(f32) + total).astype(bf16)
+        copy = send(lo.at[rows], next_ref.at[rows], "section", nxt, start=False)
+        pl.when(has_next)(copy.start)
+        next_copies.append(copy)
     for p in range(pieces):
-        finish(outs[p])
-        for rows in row_chunks:
-            cols = piece_cols[p]
-            total = reduced(out_p, out_r, rows, cols)
-            lo[rows, cols] = (x_ref[rows, cols].astype(f32) + total).astype(bf16)
-            copy = send(lo.at[rows, cols], next_ref.at[rows, cols], "section", nxt, start=False)
-            pl.when(has_next)(copy.start)
-            next_copies.append(copy)
         grads[p] = reduce_pass_on(grads[p], gq_p, gq_s, gq_r, piece_cols[p])
 
     finish(gk_copies)
@@ -538,20 +554,15 @@
             copy.wait_send()
 
 
-def hand_on(a, b, c, a_out, b_out, c_out, sem):
-    copies = [
-        pltpu.make_async_copy(src, dst, sem.at[i])
-        for i, (src, dst) in enumerate(((a, a_out), (b, b_out), (c, c_out)))
-    ]
-    for copy in copies:
-        copy.start()
-    for copy in copies:
-        copy.wait()
+def hand_on(a, b, c, a_out, b_out, c_out):
+    a_out[...] = a[...]
+    b_out[...] = b[...]
+    c_out[...] = c[...]
 
 
 def copies_needed(ways):
     if ways == 4:
-        return 1 + 9 + 3 * 4 + 2 * 6 + 2 * PIECES * 6 + 3 + 4 * PIECES
+        return 1 + 9 + 3 * 6 + 2 * 6 + 6 + PIECES * 6 + 3 + 2 + 2 * PIECES
     return 1 + (ways - 1) * (3 + 3 + 2 + 2 * PIECES + 1) + 4 * PIECES
 
 
@@ -653,13 +664,11 @@
         kv_weight[0],
         out_weight[0],
     )
-    anywhere = pl.BlockSpec(memory_space=pl.ANY)
     next_input, received, input_grad = pl.pallas_call(
         hand_on,
         out_shape=(block, block, block),
-        in_specs=[anywhere] * 3,
-        out_specs=(anywhere,) * 3,
-        scratch_shapes=[pltpu.SemaphoreType.DMA((3,))],
+        in_specs=[vmem] * 3,
+        out_specs=(vmem,) * 3,
         name="results",
     )(next_input, received, input_grad)
     return (next_input[None], received[None], input_grad[None])

time: 96.2 us -> 72.8 us (0.76)
  Pallas kernels: 94.8 us -> 71.3 us
    pallas_call x1, Pallas kernels: 25 us -> 2 us  [per_device(): pl.pallas_call(hand_on, out_shape=(block, block, block), in_specs=[vmem]...]
where the time goes in v3:
time: 72.8 us; the launch traced here: 72.6 us
  Pallas kernels  71.3 us (98%)
  between operations  1.29 us (2%)
    pallas_call x1, Pallas kernels, per_device(): pl.pallas_call(functools.partial(layer_kernel, ways, sections), out_shape...  69.3 us
    pallas_call x1, Pallas kernels, per_device(): pl.pallas_call(hand_on, out_shape=(block, block, block), in_specs=[vmem]...  2 us

profile of v3, /device:TPU:0, one launch (start us, length us, event | category | flops | bytes accessed | tf_op | source)
XLA Modules:
  0.0 72.6 jit_solution(15470284723940148570)
XLA Ops:
  1.3 69.3 %attention_layer.1 = (bf16[128,1024]{1,0:T(8,128)(2,1)}, bf16[128,1024]{1,0:T(8,128)(2,1)}, bf16[128,1024]{1,0:T(8,128)(2,1)}) custom-call(s32[1]{0:T(128)S(6)} %copy.13.slot_ref, bf16[128,1024]{1,0:T(8,128)(2,1)} %bitcast.13, bf16[2,128,1024]{2,1,0:T(8,128)(2,1)} %bitcast.12, bf16[128,1024]{1,0:T(8,128)(2,1)} %bitcast.14, f32[1,1024]{1,0:T(1,128)} %gain_ref.1, ...), custom_call_target="tpu_custom_call" | custom-call | flops 6174015488 | bytes 20971520 | tf_op jit(solution)/shard_map/attention_layer/pallas_call | solution.py:638
  70.6 2.0 %results.1 = (bf16[128,1024]{1,0:T(8,128)(2,1)}, bf16[128,1024]{1,0:T(8,128)(2,1)}, bf16[128,1024]{1,0:T(8,128)(2,1)}) custom-call(bf16[128,1024]{1,0:T(8,128)(2,1)} %get-tuple-element.9.a, bf16[128,1024]{1,0:T(8,128)(2,1)} %get-tuple-element.10.b, bf16[128,1024]{1,0:T(8,128)(2,1)} %get-tuple-element.11.c), custom_call_target="tpu_custom_call" | custom-call | tf_op jit(solution)/shard_map/results/pallas_call | solution.py:667

commit v4 on v3

--- a/solution.py
+++ b/solution.py
@@ -431,19 +431,19 @@
 
     b_far = gather_pass_on(bn, b_first)
     load_ow.wait()
-    outs = []
     for k in order:
         project(att, out_tile, out_p, out_s, k, 0, width // TILE)
-        if k == order[0]:
-            kvb = reduce_pass_on(kvb, kvb_p, kvb_p, kvb_r, kv_cols)
-        outs += reduce_send(k, out_s, out_r, all_cols)
+    kvb = reduce_pass_on(kvb, kvb_p, kvb_p, kvb_r, kv_cols)
     finish(c_second)
     finish(c_far)
     accumulate(list(range(ways)), cg, cot_block, c_acc, go, plain)
-    outs = reduce_pass_on(outs, out_p, out_s, out_r, all_cols)
     finish(b_second)
+    accumulate([0] + near, bn, query_block, b_acc)
     finish(b_far)
-    accumulate(list(range(ways)), bn, query_block, b_acc, qb, turned_query)
+    outs = []
+    for k in order:
+        outs += reduce_send(k, out_s, out_r, all_cols)
+    accumulate(far, bn, query_block, b_acc, qb, turned_query)
 
     finish(kvb)
     key, value, key_wide, value_wide = key_value(kvb_p, kvb_r)
@@ -451,6 +451,8 @@
     grad_value = jnp.zeros((tokens, HD), f32)
     mixed = jnp.zeros((tokens, HD), f32)
     for i in range(heads_here // PAIR):
+        if i == heads_here // PAIR // 2:
+            outs = reduce_pass_on(outs, out_p, out_s, out_r, all_cols)
         q = qb[PAIR * i : PAIR * (i + 1)].reshape(span, HD)
         g = go[PAIR * i : PAIR * (i + 1)].reshape(span, HD)
         probs = probabilities(q, key)

time: 72.8 us -> 73.1 us (level)
  no operation moved by 1% of the time
where the time goes in v4:
time: 73.1 us; the launch traced here: 72.9 us
  Pallas kernels  71.7 us (98%)
  between operations  1.29 us (2%)
    pallas_call x1, Pallas kernels, per_device(): pl.pallas_call(functools.partial(layer_kernel, ways, sections), out_shape...  69.7 us
    pallas_call x1, Pallas kernels, per_device(): pl.pallas_call(hand_on, out_shape=(block, block, block), in_specs=[vmem]...  2 us

profile of v4, /device:TPU:0, one launch (start us, length us, event | category | flops | bytes accessed | tf_op | source)
XLA Modules:
  0.0 72.9 jit_solution(5692836326772203938)
XLA Ops:
  1.3 69.7 %attention_layer.1 = (bf16[128,1024]{1,0:T(8,128)(2,1)}, bf16[128,1024]{1,0:T(8,128)(2,1)}, bf16[128,1024]{1,0:T(8,128)(2,1)}) custom-call(s32[1]{0:T(128)S(6)} %copy.13.slot_ref, bf16[128,1024]{1,0:T(8,128)(2,1)} %bitcast.13, bf16[2,128,1024]{2,1,0:T(8,128)(2,1)} %bitcast.12, bf16[128,1024]{1,0:T(8,128)(2,1)} %bitcast.14, f32[1,1024]{1,0:T(1,128)} %gain_ref.1, ...), custom_call_target="tpu_custom_call" | custom-call | flops 6174015488 | bytes 20971520 | tf_op jit(solution)/shard_map/attention_layer/pallas_call | solution.py:640
  70.9 2.0 %results.1 = (bf16[128,1024]{1,0:T(8,128)(2,1)}, bf16[128,1024]{1,0:T(8,128)(2,1)}, bf16[128,1024]{1,0:T(8,128)(2,1)}) custom-call(bf16[128,1024]{1,0:T(8,128)(2,1)} %get-tuple-element.9.a, bf16[128,1024]{1,0:T(8,128)(2,1)} %get-tuple-element.10.b, bf16[128,1024]{1,0:T(8,128)(2,1)} %get-tuple-element.11.c), custom_call_target="tpu_custom_call" | custom-call | tf_op jit(solution)/shard_map/results/pallas_call | solution.py:669

commit v5 on v4

--- a/solution.py
+++ b/solution.py
@@ -105,6 +105,7 @@
     gl,
     f_sum,
     b_sum,
+    t_sum,
     m_sum,
     wsem,
     ssem,
@@ -150,7 +151,7 @@
             dst_ref=dst,
             send_sem=ssem.at[i],
             recv_sem=rsem.at[i],
-            device_id={axis: peer},
+            device_id=axis if peer is None else {axis: peer},
             device_id_type=pl.DeviceIdType.MESH,
         )
         if start:
@@ -170,7 +171,13 @@
 
     for k in range(1, ways):
         greet("tensor", peers[k])
-    greet("section", mirror)
+    for k in range(ways):
+        pl.semaphore_signal(
+            barrier,
+            inc=1,
+            device_id={"section": mirror, "tensor": peers[k]},
+            device_id_type=pl.DeviceIdType.MESH,
+        )
 
     @pl.when(has_prev)
     def _():
@@ -216,15 +223,14 @@
             total = total + buf[k, 0:1, :]
         return jnp.sum(jnp.where(eye, total, 0.0), axis=1, keepdims=True)
 
-    def normalize(rows_ref, out, total):
-        factor = lax.rsqrt(total / model + norm_eps)
-        for r in range(0, tokens, step):
+    def normalize(rows_ref, out, factor, first, last):
+        for r in range(first, last, step):
             v = rows_ref[r : r + step, :].astype(f32)
             out[0, r : r + step, :] = (v * factor[r : r + step] * gain_ref[...]).astype(bf16)
-        return factor
 
     sum_put(squares(x_ref), f_sum)
-    pl.semaphore_wait(barrier, ways + jnp.minimum(sec, 1) + jnp.minimum(sections - 1 - sec, 1))
+    sum_put(squares(trav), t_sum)
+    pl.semaphore_wait(barrier, 2 * ways - 1 + jnp.minimum(sec, 1) + jnp.minimum(sections - 1 - sec, 1))
 
     def gather_first(buf):
         if relay:
@@ -384,10 +390,17 @@
         rows = pl.ds(pl.multiple_of(peers[k] * width + n * TILE, TILE), TILE)
         return dot_nt(source[...], qw[rows, :])
 
-    travel_copy = send(trav, travel_ref, "section", mirror)
+    travel_copies = [
+        send(trav.at[rows], travel_ref.at[rows], "section", mirror) for rows in (upper, lower)
+    ]
     f_sums = sum_send(f_sum)
+    b_sums = [
+        send(t_sum.at[0], b_sum.at[k], {"section": mirror, "tensor": peers[k]}, None)
+        for k in range(ways)
+    ]
     c_first = gather_first(cg)
-    normalize(x_ref, fn, sum_total(f_sums, f_sum))
+    f_total = sum_total(f_sums, f_sum)
+    normalize(x_ref, fn, lax.rsqrt(f_total / model + norm_eps), 0, tokens)
     x_first = gather_first(fn)
     x_second = gather_second(fn)
     load_kvw.wait()
@@ -398,27 +411,38 @@
     c_far = gather_pass_on(cg, c_first)
     c_second = gather_second(cg)
     kvf = reduce_pass_on(kvf, kvf_p, kvf_p, kvf_r, kv_cols)
+    b_total = jnp.where(early, sum_total(b_sums, b_sum), f_total)
+    factor = lax.rsqrt(b_total / model + norm_eps)
+
+    def take_back(copy, rows, first):
+        copy.wait_recv()
+
+        @pl.when(early)
+        def _():
+            back[rows, :] = travel_ref[rows, :]
+
+        @pl.when(jnp.logical_not(early))
+        def _():
+            back[rows, :] = x_ref[rows, :]
+
+        normalize(back, bn, factor, first, first + half)
+
+    take_back(travel_copies[0], upper, 0)
+    if relay:
+        b_first = [to_peer(1, bn.at[0, upper], bn.at[1, upper])]
+        b_second = [to_peer(2, bn.at[0, upper], bn.at[2, upper])]
     finish(x_second)
     accumulate(near, fn, query_block, f_acc)
-
-    travel_copy.wait_recv()
-
-    @pl.when(early)
-    def _():
-        back[...] = travel_ref[...]
-
-    @pl.when(jnp.logical_not(early))
-    def _():
-        back[...] = x_ref[...]
-
-    sum_put(squares(back), b_sum)
-    b_sums = sum_send(b_sum)
+    take_back(travel_copies[1], lower, half)
+    if relay:
+        b_first.append(to_peer(2, bn.at[0, lower], bn.at[2, lower]))
+        b_second.append(to_peer(1, bn.at[0, lower], bn.at[1, lower]))
+    else:
+        b_first = gather_first(bn)
+        b_second = []
+    kvb = kv_terms(bn, kvb_p, kvb_r)
     finish(x_far)
     accumulate(far, fn, query_block, f_acc, qf, turned_query)
-    factor = normalize(back, bn, sum_total(b_sums, b_sum))
-    b_first = gather_first(bn)
-    b_second = gather_second(bn)
-    kvb = kv_terms(bn, kvb_p, kvb_r)
     finish(kvf)
     key, value, _, _ = key_value(kvf_p, kvf_r)
     for i in range(heads_here // PAIR):
@@ -564,8 +588,8 @@
 
 def copies_needed(ways):
     if ways == 4:
-        return 1 + 9 + 3 * 6 + 2 * 6 + 6 + PIECES * 6 + 3 + 2 + 2 * PIECES
-    return 1 + (ways - 1) * (3 + 3 + 2 + 2 * PIECES + 1) + 4 * PIECES
+        return 2 + 6 + 4 + 3 * 6 + 2 * 6 + 6 + PIECES * 6 + 3 + 2 + 2 * PIECES
+    return 3 + (ways - 1) * (3 + 3 + 2 + 2 * PIECES + 1) + 4 * PIECES
 
 
 def per_device(
@@ -631,6 +655,7 @@
         flat_block,
         sums,
         sums,
+        pltpu.VMEM((1, SUMROWS, tokens), f32),
         sums,
         pltpu.SemaphoreType.DMA((3,)),
         pltpu.SemaphoreType.DMA((copies,)),

time: 73.1 us -> 73.7 us (level)
  no operation moved by 1% of the time
where the time goes in v5:
time: 73.7 us; the launch traced here: 73.5 us
  Pallas kernels  72.2 us (98%)
  between operations  1.29 us (2%)
    pallas_call x1, Pallas kernels, per_device(): pl.pallas_call(functools.partial(layer_kernel, ways, sections), out_shape...  70.2 us
    pallas_call x1, Pallas kernels, per_device(): pl.pallas_call(hand_on, out_shape=(block, block, block), in_specs=[vmem]...  2 us

profile of v5, /device:TPU:0, one launch (start us, length us, event | category | flops | bytes accessed | tf_op | source)
XLA Modules:
  0.0 73.5 jit_solution(12981187317599473729)
XLA Ops:
  1.3 70.2 %attention_layer.1 = (bf16[128,1024]{1,0:T(8,128)(2,1)}, bf16[128,1024]{1,0:T(8,128)(2,1)}, bf16[128,1024]{1,0:T(8,128)(2,1)}) custom-call(s32[1]{0:T(128)S(6)} %copy.13.slot_ref, bf16[128,1024]{1,0:T(8,128)(2,1)} %bitcast.13, bf16[2,128,1024]{2,1,0:T(8,128)(2,1)} %bitcast.12, bf16[128,1024]{1,0:T(8,128)(2,1)} %bitcast.14, f32[1,1024]{1,0:T(1,128)} %gain_ref.1, ...), custom_call_target="tpu_custom_call" | custom-call | flops 6174015488 | bytes 20971520 | tf_op jit(solution)/shard_map/attention_layer/pallas_call | solution.py:665
  71.5 2.0 %results.1 = (bf16[128,1024]{1,0:T(8,128)(2,1)}, bf16[128,1024]{1,0:T(8,128)(2,1)}, bf16[128,1024]{1,0:T(8,128)(2,1)}) custom-call(bf16[128,1024]{1,0:T(8,128)(2,1)} %get-tuple-element.9.a, bf16[128,1024]{1,0:T(8,128)(2,1)} %get-tuple-element.10.b, bf16[128,1024]{1,0:T(8,128)(2,1)} %get-tuple-element.11.c), custom_call_target="tpu_custom_call" | custom-call | tf_op jit(solution)/shard_map/results/pallas_call | solution.py:694
